TPU v7x, 128 devices: a whole 4x4x4 slice. The times are simulated.
128 devices in a mesh: dp: 16 (over x, z_lo, core), vocab: 8 (over y, z_hi).
Axes of the slice: x: 4, y: 4, z: 4 (z_hi: 2, z_lo: 2; z = z_hi * 2 + z_lo), core: 2. Of those that a mesh axis runs over, the one named last changes fastest.
Arguments:
- hidden_states: bfloat16 [32768, 4096], P('dp'), may hold values from -6 to 6
- logit_grads: bfloat16 [32768, 12288], P('dp', 'vocab'), may hold values from -0.03125 to 0.03125
- master: float32 [8, 1536, 4096], P('vocab', 'dp'), may hold values from -0.006 to 0.006
- moment_one: float32 [8, 1536, 4096], P('vocab', 'dp'), may hold values from -4 to 4
- moment_two: float32 [8, 1536, 4096], P('vocab', 'dp'), may hold values from 0.0001 to 0.01
Outputs:
- new_master: float32 [8, 1536, 4096], P('vocab', 'dp')
- new_moment_one: float32 [8, 1536, 4096], P('vocab', 'dp')
- new_moment_two: float32 [8, 1536, 4096], P('vocab', 'dp')
- sampler_head: bfloat16 [12288, 4096], P(None, 'vocab')
All inputs are finite; a program needn't handle non-finite values.
Results may differ from a plain program's by a relative error of at most 0.001.
Values may be sent and summed in bfloat16 or wider, within the bound.
No kernel may reach another device: no remote copies, remote signals or barrier semaphores. Data moves between devices by JAX's collectives and lax.ppermute only.
A program may use at most 192 MiB of HBM per device.

v0:
```python
import jax
import jax.numpy as jnp
from jax import lax
from jax.experimental import pallas as pl
from jax.experimental.pallas import tpu as pltpu
from jax.sharding import Mesh, PartitionSpec as P

STEP = 100

beta_one = 0.9
beta_two = 0.999
learn_rate = 0.001
decay_rate = 0.1
epsilon = 1e-08

F16 = jnp.float16
F32 = jnp.float32
BF16 = jnp.bfloat16


def params(mib):
    return pltpu.CompilerParams(vmem_limit_bytes=mib * 2**20)


SWAP = [(0, 1), (1, 0)]
SWAPS = [[(2 * x + c, 2 * (x ^ (1 if c == k else 3)) + c) for x in range(4) for c in range(2)] for k in range(2)]

CHUNKS = (48, 48)
STARTS = (0, 48)


def order_kernel(where, grads, *outs):
    z, c = where[1], where[2]
    for block in range(3):
        turned = grads[:, 128 * block : 128 * block + 128].T
        for q in range(8):
            row = 128 * block + 16 * q
            owner, at = row // 96, row % 96
            piece = turned[16 * q : 16 * q + 16]
            same = jnp.where(z == owner // 2, 1, 0)
            start = 0
            for k, count in enumerate(CHUNKS):
                if start <= at < start + count:
                    for keep in range(2):

                        @pl.when((c == owner % 2) == (keep == 1))
                        def _():
                            outs[2 * k + keep][0, same, at - start : at - start + 16, :] = piece

                start += count


def order_rows(where, logit_grads):
    def block(i, s):
        x, core = s[0], s[2]
        one, three = x + 1 - 2 * (x % 2), 3 - x
        first = jnp.where(core == 0, one, three)
        second = jnp.where(core == 0, three, one)
        return jnp.where(i == 0, (x + 2) % 4, jnp.where(i == 1, first, jnp.where(i == 2, second, x)))

    return pl.pallas_call(
        order_kernel,
        grid_spec=pltpu.PrefetchScalarGridSpec(
            num_scalar_prefetch=1,
            grid=(4,),
            in_specs=[pl.BlockSpec((2048, 384), lambda i, s: (0, block(i, s)))],
            out_specs=[
                pl.BlockSpec((1, 2, count, 2048), index)
                for count in CHUNKS
                for index in (
                    lambda i, s: (jnp.where((i == 1) | (i == 2), 3 - i, i), 0, 0, 0),
                    lambda i, s: (i, 0, 0, 0),
                )
            ],
        ),
        out_shape=[jax.ShapeDtypeStruct((4, 2, count, 2048), BF16) for count in CHUNKS for _ in range(2)],
        compiler_params=params(14),
        name="order_rows",
    )(where, logit_grads)


def adam_kernel(first_group, where, gradient, master, one, two, *rest):
    new_master, new_one, new_two, rounded = rest if first_group else rest[3:]
    g = gradient[...]
    m = beta_one * one[...] + (1.0 - beta_one) * g
    v = beta_two * two[...] + (1.0 - beta_two) * g * g
    first_hat = m / (1.0 - beta_one**STEP)
    second_hat = v / (1.0 - beta_two**STEP)
    old = master[...]
    new = old - learn_rate * (first_hat / (jnp.sqrt(second_hat) + epsilon) + decay_rate * old)
    new_master[...] = new
    new_one[...] = m
    new_two[...] = v
    rounded[where[4], 0] = new[:, :512].astype(BF16)
    rounded[1 - where[4], 0] = new[:, 512:].astype(BF16)


def adam(where, gradient, state, outs, group):
    rows, at = CHUNKS[group], STARTS[group] // CHUNKS[group]
    tile = pl.BlockSpec((rows, 1024), lambda w, s: (at, w))
    given = () if outs is None else outs
    got = pl.pallas_call(
        lambda *refs: adam_kernel(outs is None, *refs),
        grid_spec=pltpu.PrefetchScalarGridSpec(
            num_scalar_prefetch=1,
            grid=(4,),
            in_specs=[pl.BlockSpec((rows, 1024), lambda w, s: (0, w)), tile, tile, tile]
            + [pl.BlockSpec(memory_space=pl.ANY)] * len(given),
            out_specs=[tile] * 3 + [pl.BlockSpec((2, 1, rows, 512), lambda w, s: (0, (w + 4 - s[3]) % 4, 0, 0))],
        ),
        out_shape=[jax.ShapeDtypeStruct((96, 4096), F32)] * 3 + [jax.ShapeDtypeStruct((2, 4, rows, 512), BF16)],
        input_output_aliases={} if outs is None else {5: 0, 6: 1, 7: 2},
        compiler_params=params(6),
        name=f"adam_{group}",
    )(where, gradient, *state, *given)
    return got[:3], got[3]


def exchange(where, rounded, gate):
    rows = rounded.shape[2]
    got = after(lax.ppermute(rounded[1], "zh", SWAP), *gate)
    came = [
        lax.ppermute(jnp.stack([rounded[0, k], got[k]]), "y", [(i, (i + k) % 4) for i in range(4)]) for k in (1, 2, 3)
    ]

    def kernel(where, rounded, got, one, two, three, out, sem):
        copies = []
        for k, pair in enumerate(((rounded.at[0, 0], got.at[0]), *((a.at[0], a.at[1]) for a in (one, two, three)))):
            for r, source in enumerate(pair):
                block = (where[3] + 4 - k) % 4 * 2 + (where[4] + r) % 2
                copies.append(pltpu.make_async_copy(source, out.at[block], sem.at[2 * k + r]))
        for copy in copies:
            copy.start()
        for copy in copies:
            copy.wait()

    whole = pl.BlockSpec(memory_space=pl.ANY)
    return pl.pallas_call(
        kernel,
        grid_spec=pltpu.PrefetchScalarGridSpec(
            num_scalar_prefetch=1,
            grid=(1,),
            in_specs=[whole] * 5,
            out_specs=whole,
            scratch_shapes=[pltpu.SemaphoreType.DMA((8,))],
        ),
        out_shape=jax.ShapeDtypeStruct((8, rows, 512), BF16),
        compiler_params=params(1),
        name="collect",
    )(where, rounded, got, *came)


def place(where, arrays, pieces, head, group):
    given = () if head is None else (head,)

    def kernel(where, *refs):
        out, mark, sem = refs[-3:]
        copies = []
        x = where[0]
        one, three = x + 1 - 2 * (x % 2), 3 - x
        for k, (source, first, (at, z, c)) in enumerate(pieces):
            core = (where[2] + c) % 2
            from_x = (x, jnp.where(core == 0, three, one), jnp.where(core == 0, one, three), (x + 2) % 4)[at]
            dp = from_x * 4 + (where[1] + z) % 2 * 2 + core
            copies.append(
                pltpu.make_async_copy(
                    refs[source].at[pl.ds(first, 8)],
                    out.at[:, dp, pl.ds(STARTS[group], CHUNKS[group]), :],
                    sem.at[k],
                )
            )
        for copy in copies:
            copy.start()
        mark[...] = jnp.zeros_like(mark)
        for copy in copies:
            copy.wait()

    whole = pl.BlockSpec(memory_space=pl.ANY)
    return pl.pallas_call(
        kernel,
        grid_spec=pltpu.PrefetchScalarGridSpec(
            num_scalar_prefetch=1,
            grid=(1,),
            in_specs=[whole] * (len(arrays) + len(given)),
            out_specs=[whole, pl.BlockSpec((8, 128), lambda i, s: (0, 0))],
            scratch_shapes=[pltpu.SemaphoreType.DMA((len(pieces),))],
        ),
        out_shape=[jax.ShapeDtypeStruct((8, 16, 96, 512), BF16), jax.ShapeDtypeStruct((8, 128), F32)],
        input_output_aliases={} if head is None else {1 + len(arrays): 0},
        compiler_params=params(1),
        name=f"place_{group}",
    )(where, *arrays, *given)


def after(value, *others):
    if not others:
        return value

    def kernel(*refs):
        pass

    others = [a[:8, :128].astype(F32) if a.dtype == F16 else a for a in others]
    whole = pl.BlockSpec(memory_space=pl.ANY)
    return pl.pallas_call(
        kernel,
        in_specs=[whole] * (1 + len(others)),
        out_specs=whole,
        out_shape=jax.ShapeDtypeStruct(value.shape, value.dtype),
        input_output_aliases={0: 0},
        compiler_params=params(1),
        name="after",
    )(value, *others)


def wide(a):
    return a.astype(F32)


def dot(a, b):
    return jnp.dot(a, b, preferred_element_type=F32)


def swap(a, k):
    return lax.ppermute(a, ("x", "c"), SWAPS[k])


def gather(where, mine, head, group, marks, gate):
    side = lax.ppermute(mine, "zl", SWAP)
    for z, own in enumerate((mine, side)):
        pair = jnp.concatenate([own, swap(own, 1)], 0)
        far = swap(after(pair, *gate) if z == 0 else pair, 0)
        for at, a in ((0, pair), (2, far)):
            if group == 1 and z == 1 and at == 2:
                a = after(a, *marks)
            pieces = [(c, 8 * k, (at + k, z, c)) for c in range(2) for k in range(2)]
            head, mark = place(where, (a, lax.ppermute(a, "c", SWAP)), pieces, head, group)
            marks = marks + [mark]
    return head, marks, pair


def local(hidden_states, logit_grads, master, moment_one, moment_two):
    where = jnp.stack([lax.axis_index(a) for a in ("x", "zl", "c", "y", "zh")]).astype(jnp.int32)
    rows = order_rows(where, logit_grads)
    rows = [a.reshape(-1, 2048) for a in rows]

    def send_first(keep, came):
        n = keep.shape[0] // 2
        sent = (keep[:n] + wide(came[:n])).astype(F16)
        return swap(sent, 0), sent

    def send_second(keep, came, got, after_this):
        n = keep.shape[0] // 4
        total = keep[2 * n : 3 * n] + wide(came[2 * n : 3 * n]) + wide(got[:n])
        if after_this is not None:
            total = total + after_this.reshape(-1)[:1].astype(F32)[:, None] * 0
        sent = total.astype(F16)
        return swap(sent, 1), sent

    def send_side(keep, came, got, last):
        n = keep.shape[0] // 4
        own = keep[3 * n :] + wide(came[3 * n :]) + wide(got[n:]) + wide(last)
        return own[n // 2 :] + wide(lax.ppermute(own[: n // 2].astype(F16), "zl", SWAP)), own

    def update(gradient, outs, group, gate):
        outs, rounded = adam(where, gradient, (master[0], moment_one[0], moment_two[0]), outs, group)
        return outs, exchange(where, rounded, gate)

    came_a = lax.ppermute(dot(rows[0], hidden_states).astype(F16), "c", SWAP)
    keep_a = dot(rows[1], hidden_states)
    first_a, _ = send_first(keep_a, came_a)
    came_b = lax.ppermute(dot(after(rows[2], keep_a), hidden_states).astype(F16), "c", SWAP)
    second_a, sent = send_second(keep_a, came_a, first_a, None)
    keep_b = dot(after(rows[3], sent), hidden_states)
    first_b, sent = send_first(keep_b, came_b)
    gradient, _ = send_side(keep_a, came_a, first_a, second_a)
    outs, mine = update(after(gradient, sent), None, 0, ())
    second_b, _ = send_second(keep_b, came_b, first_b, None)
    gradient, own = send_side(keep_b, came_b, first_b, second_b)
    head, marks, pair = gather(where, mine, None, 0, [], (own,))
    outs, mine = update(gradient, outs, 1, (pair,))
    head, _, _ = gather(where, mine, head, 1, marks, ())
    return (*(o[None] for o in outs), head.reshape(12288, 512))


def solution(mesh):
    parts = Mesh(mesh.devices.reshape(4, 2, 2, 4, 2), ("x", "zl", "c", "y", "zh"))
    dp, vocab = ("x", "zl", "c"), ("y", "zh")
    held = P(vocab, dp, None)
    return jax.shard_map(
        local,
        mesh=parts,
        in_specs=(P(dp, None), P(dp, vocab), held, held, held),
        out_specs=(held, held, held, P(None, vocab)),
        check_vma=False,
    )
```

profile of v0, /device:TPU:1, one launch (start us, length us, event | category | flops | bytes accessed | tf_op | source)
XLA Modules:
  0.0 189.1 jit_solution(10478101320314955931)
XLA Ops:
  0.7 2.8 %copy-done = bf16[2048,1536]{1,0:T(8,128)(2,1)S(1)} copy-done((bf16[2048,1536]{1,0:T(8,128)(2,1)S(1)}, bf16[2048,1536]{1,0:T(8,128)(2,1)}, u32[]{:S(2)}) %copy-start) | copy-done | bytes 6291480
  3.5 4.5 %order_rows.1 = (bf16[4,2,48,2048]{3,2,1,0:T(8,128)(2,1)S(1)}, bf16[4,2,48,2048]{3,2,1,0:T(8,128)(2,1)S(1)}, bf16[4,2,48,2048]{3,2,1,0:T(8,128)(2,1)S(1)}, bf16[4,2,48,2048]{3,2,1,0:T(8,128)(2,1)S(1)}) custom-call(s32[5]{0:T(128)S(1)} %stack.41.where.refs_0_, bf16[2048,1536]{1,0:T(8,128)(2,1)S(1)} %copy-done), custom_call_target="tpu_custom_call" | custom-call | tf_op jit(solution)/shard_map/order_rows/pallas_call | solution.py:61
  8.1 10.3 %convolution_convert_fusion.1 = f16[384,4096]{1,0:T(8,128)(2,1)S(1)} fusion(bf16[384,2048]{1,0:T(8,128)(2,1)S(1)} %bitcast.49, bf16[2048,4096]{1,0:T(8,128)(2,1)} %param.5), kind=kOutput, calls=%fused_computation.1 | convolution fusion | flops 6444023808 | bytes 21495808 | tf_op jit(solution)/shard_map/dot_general | solution.py:220
  18.4 1.5 collective-permute-start
  19.8 10.3 %fusion.12.refs_1_ = f32[384,4096]{1,0:T(8,128)S(1)} fusion(bf16[384,2048]{1,0:T(8,128)(2,1)S(1)} %bitcast.48, bf16[2048,4096]{1,0:T(8,128)(2,1)} %param.5), kind=kOutput, calls=%fused_computation.46 | convolution fusion | flops 6442450944 | bytes 24641536 | tf_op jit(solution)/shard_map/dot_general | solution.py:220
  30.6 2.6 %collective-permute-start.1 = (f16[192,4096]{1,0:T(8,128)(2,1)S(1)}, f16[192,4096]{1,0:T(8,128)(2,1)S(1)}, u32[]{:S(2)}, u32[]{:S(2)}) collective-permute-start(f16[192,4096]{1,0:T(8,128)(2,1)S(1)} %fusion.1), channel_id=1, source_target_pairs={{0,32},{8,104},{32,0},{40,72},{64,96},{72,40},{96,64},{104,8},{1,3... | collective-permute-start | bytes 4718600 | tf_op jit(solution)/shard_map/ppermute | solution.py:224
  33.2 10.3 %convolution_convert_fusion = f16[384,4096]{1,0:T(8,128)(2,1)S(1)} fusion(bf16[384,2048]{1,0:T(8,128)(2,1)S(1)} %after.7, bf16[2048,4096]{1,0:T(8,128)(2,1)} %param.5), kind=kOutput, calls=%fused_computation | convolution fusion | flops 6444023808 | bytes 21495808 | tf_op jit(solution)/shard_map/dot_general | solution.py:220
  43.6 7.5 %collective-permute-done.1 = f16[192,4096]{1,0:T(8,128)(2,1)S(1)} collective-permute-done((f16[192,4096]{1,0:T(8,128)(2,1)S(1)}, f16[192,4096]{1,0:T(8,128)(2,1)S(1)}, u32[]{:S(2)}, u32[]{:S(2)}) %collective-permute-start.1) | collective-permute-done | bytes 1572896 | tf_op jit(solution)/shard_map/ppermute | solution.py:224
  52.1 10.3 %fusion.13 = f32[384,4096]{1,0:T(8,128)S(1)} fusion(bf16[384,2048]{1,0:T(8,128)(2,1)S(1)} %after.6, bf16[2048,4096]{1,0:T(8,128)(2,1)} %param.5), kind=kOutput, calls=%fused_computation.47 | convolution fusion | flops 6442450944 | bytes 24641536 | tf_op jit(solution)/shard_map/dot_general | solution.py:220
  63.3 1.8 collective-permute-start.7
  65.5 2.6 %collective-permute-start.3 = (f16[192,4096]{1,0:T(8,128)(2,1)S(1)}, f16[192,4096]{1,0:T(8,128)(2,1)S(1)}, u32[]{:S(2)}, u32[]{:S(2)}) collective-permute-start(f16[192,4096]{1,0:T(8,128)(2,1)S(1)} %fusion), channel_id=1, source_target_pairs={{0,32},{8,104},{32,0},{40,72},{64,96},{72,40},{96,64},{104,8},{1,3... | collective-permute-start | bytes 4718600 | tf_op jit(solution)/shard_map/ppermute | solution.py:224
  68.1 4.4 %collective-permute-done.7 = f16[48,4096]{1,0:T(8,128)(2,1)S(1)} collective-permute-done((f16[48,4096]{1,0:T(8,128)(2,1)S(1)}, f16[48,4096]{1,0:T(8,128)(2,1)S(1)}, u32[]{:S(2)}, u32[]{:S(2)}) %collective-permute-start.7) | collective-permute-done | bytes 393248 | tf_op jit(solution)/shard_map/ppermute | solution.py:262
  72.6 2.9 %adam_0.1 = (f32[96,4096]{1,0:T(8,128)}, f32[96,4096]{1,0:T(8,128)}, f32[96,4096]{1,0:T(8,128)}, bf16[2,4,48,512]{3,2,1,0:T(8,128)(2,1)S(1)}) custom-call(s32[5]{0:T(128)S(1)} %stack.41.where.refs_0_, f32[48,4096]{1,0:T(8,128)S(1)} %after.8.refs_1_, f32[96,4096]{1,0:T(8,128)S(1)} %bitcast.40, f32[96,4096]{1,0:T(8,128)S(1)} %bitcast.42, f32[96,4096]{1,0:T(8,128)S(1)} %bitcast.44), custom_call_target="tpu_custom_call" | custom-call | tf_op jit(solution)/shard_map/adam_0/pallas_call | solution.py:102
  75.5 3.2 %collective-permute-start.9 = (bf16[4,48,512]{2,1,0:T(8,128)(2,1)S(1)}, bf16[4,48,512]{2,1,0:T(8,128)(2,1)S(1)}, u32[]{:S(2)}, u32[]{:S(2)}) collective-permute-start(bf16[4,48,512]{2,1,0:T(8,128)(2,1)S(1)} %slice_bitcast_fusion), channel_id=1, source_target_pairs={{0,1},{1,0},{2,3},{3,2},{4,5},{5,4},{6,7},{7,6},{8,9},{9,8},{10,11... | collective-permute-start | bytes 589832 | tf_op jit(solution)/shard_map/ppermute | solution.py:121
  78.7 3.0 %collective-permute-done.9.got = bf16[4,48,512]{2,1,0:T(8,128)(2,1)S(1)} collective-permute-done((bf16[4,48,512]{2,1,0:T(8,128)(2,1)S(1)}, bf16[4,48,512]{2,1,0:T(8,128)(2,1)S(1)}, u32[]{:S(2)}, u32[]{:S(2)}) %collective-permute-start.9) | collective-permute-done | bytes 196640 | tf_op jit(solution)/shard_map/ppermute | solution.py:121
  81.8 1.4 collective-permute-start.10
  83.2 2.9 %collective-permute-done.3 = f16[192,4096]{1,0:T(8,128)(2,1)S(1)} collective-permute-done((f16[192,4096]{1,0:T(8,128)(2,1)S(1)}, f16[192,4096]{1,0:T(8,128)(2,1)S(1)}, u32[]{:S(2)}, u32[]{:S(2)}) %collective-permute-start.3) | collective-permute-done | bytes 1572896 | tf_op jit(solution)/shard_map/ppermute | solution.py:224
  86.6 3.0 %collective-permute-start.11 = (bf16[2,48,512]{2,1,0:T(8,128)(2,1)S(1)}, bf16[2,48,512]{2,1,0:T(8,128)(2,1)S(1)}, u32[]{:S(2)}, u32[]{:S(2)}) collective-permute-start(bf16[2,48,512]{2,1,0:T(8,128)(2,1)S(1)} %pad_maximum_fusion.3), channel_id=1, source_target_pairs={{0,4},{2,6},{4,0},{6,2},{1,5},{3,7},{5,1},{7,3},{8,12},{10,14},{12... | collective-permute-start | bytes 294920 | tf_op jit(solution)/shard_map/ppermute | solution.py:123
  90.4 1.9 collective-permute-done.11.two
  92.3 1.1 collective-permute-done.12.three
  93.4 1.2 collect.2
  94.6 1.4 collective-permute-start.21
  96.2 5.3 %collective-permute-done.21 = bf16[8,48,512]{2,1,0:T(8,128)(2,1)S(1)} collective-permute-done((bf16[8,48,512]{2,1,0:T(8,128)(2,1)S(1)}, bf16[8,48,512]{2,1,0:T(8,128)(2,1)S(1)}, u32[]{:S(2)}, u32[]{:S(2)}) %collective-permute-start.21) | collective-permute-done | bytes 393248 | tf_op jit(solution)/shard_map/ppermute | solution.py:224
  101.6 8.3 %collective-permute-start.22 = (bf16[16,48,512]{2,1,0:T(8,128)(2,1)S(1)}, bf16[16,48,512]{2,1,0:T(8,128)(2,1)S(1)}, u32[]{:S(2)}, u32[]{:S(2)}) collective-permute-start(bf16[16,48,512]{2,1,0:T(8,128)(2,1)S(1)} %pad_maximum_fusion.refs_0_), channel_id=1, source_target_pairs={{0,8},{8,0},{1,9},{9,1},{2,10},{10,2},{3,11},{11,3},{4,12},{12,4},... | collective-permute-start | bytes 2359304 | tf_op jit(solution)/shard_map/ppermute | solution.py:236
  110.4 6.3 %collective-permute-done.14 = bf16[8,48,512]{2,1,0:T(8,128)(2,1)S(1)} collective-permute-done((bf16[8,48,512]{2,1,0:T(8,128)(2,1)S(1)}, bf16[8,48,512]{2,1,0:T(8,128)(2,1)S(1)}, u32[]{:S(2)}, u32[]{:S(2)}) %collective-permute-start.14) | collective-permute-done | bytes 393248 | tf_op jit(solution)/shard_map/ppermute | solution.py:224
  116.8 1.7 place_0.4
  119.2 2.9 %adam_1.1 = (f32[96,4096]{1,0:T(8,128)}, f32[96,4096]{1,0:T(8,128)}, f32[96,4096]{1,0:T(8,128)}, bf16[2,4,48,512]{3,2,1,0:T(8,128)(2,1)S(1)}) custom-call(s32[5]{0:T(128)S(1)} %stack.41.where.refs_0_, f32[48,4096]{1,0:T(8,128)S(1)} %slice_add_fusion.7.refs_1_, f32[96,4096]{1,0:T(8,128)S(1)} %bitcast.41, ...), custom_call_target="tpu_custom_call", output_to_operand_aliasing={{0}: (5, {}), {1}: (6, {}), {2}: (7, {})} | custom-call | tf_op jit(solution)/shard_map/adam_1/pallas_call | solution.py:102
  122.1 3.4 %collective-permute-start.8 = (bf16[4,48,512]{2,1,0:T(8,128)(2,1)S(1)}, bf16[4,48,512]{2,1,0:T(8,128)(2,1)S(1)}, u32[]{:S(2)}, u32[]{:S(2)}) collective-permute-start(bf16[4,48,512]{2,1,0:T(8,128)(2,1)S(1)} %slice_bitcast_fusion.1), channel_id=1, source_target_pairs={{0,1},{1,0},{2,3},{3,2},{4,5},{5,4},{6,7},{7,6},{8,9},{9,8},{10,11... | collective-permute-start | bytes 589832 | tf_op jit(solution)/shard_map/ppermute | solution.py:121
  125.5 3.0 %collective-permute-done.8.refs_0_ = bf16[4,48,512]{2,1,0:T(8,128)(2,1)S(1)} collective-permute-done((bf16[4,48,512]{2,1,0:T(8,128)(2,1)S(1)}, bf16[4,48,512]{2,1,0:T(8,128)(2,1)S(1)}, u32[]{:S(2)}, u32[]{:S(2)}) %collective-permute-start.8) | collective-permute-done | bytes 196640 | tf_op jit(solution)/shard_map/ppermute | solution.py:121
  128.9 2.7 %collective-permute-start.16 = (bf16[2,48,512]{2,1,0:T(8,128)(2,1)S(1)}, bf16[2,48,512]{2,1,0:T(8,128)(2,1)S(1)}, u32[]{:S(2)}, u32[]{:S(2)}) collective-permute-start(bf16[2,48,512]{2,1,0:T(8,128)(2,1)S(1)} %pad_maximum_fusion.6), channel_id=1, source_target_pairs={{0,4},{2,6},{4,0},{6,2},{1,5},{3,7},{5,1},{7,3},{8,12},{10,14},{12... | collective-permute-start | bytes 294920 | tf_op jit(solution)/shard_map/ppermute | solution.py:123
  132.2 1.1 collective-permute-done.15.one
  133.3 1.3 collective-permute-done.16.two
  135.2 1.2 collect.3
  136.3 6.8 %collective-permute-start.28 = (bf16[8,48,512]{2,1,0:T(8,128)(2,1)S(1)}, bf16[8,48,512]{2,1,0:T(8,128)(2,1)S(1)}, u32[]{:S(2)}, u32[]{:S(2)}) collective-permute-start(bf16[8,48,512]{2,1,0:T(8,128)(2,1)S(1)} %collect.3), channel_id=1, source_target_pairs={{0,96},{8,40},{32,64},{40,8},{64,32},{72,104},{96,0},{104,72},{1,9... | collective-permute-start | bytes 1179656 | tf_op jit(solution)/shard_map/ppermute | solution.py:224
  143.2 7.2 %collective-permute-done.28 = bf16[8,48,512]{2,1,0:T(8,128)(2,1)S(1)} collective-permute-done((bf16[8,48,512]{2,1,0:T(8,128)(2,1)S(1)}, bf16[8,48,512]{2,1,0:T(8,128)(2,1)S(1)}, u32[]{:S(2)}, u32[]{:S(2)}) %collective-permute-start.28) | collective-permute-done | bytes 393248 | tf_op jit(solution)/shard_map/ppermute | solution.py:224
  150.5 6.8 %collective-permute-start.25 = (bf16[16,48,512]{2,1,0:T(8,128)(2,1)S(1)}, bf16[16,48,512]{2,1,0:T(8,128)(2,1)S(1)}, u32[]{:S(2)}, u32[]{:S(2)}) collective-permute-start(bf16[16,48,512]{2,1,0:T(8,128)(2,1)S(1)} %constant_dynamic-update-slice_fusion.refs_1_.refs_0_), channel_id=1, source_target_pairs={{0,8},{8,0},{1,9},{9,1},{2,10},{10,2},{3,11},{11,3},{4,12},{12,4},... | collective-permute-start | bytes 2359304 | tf_op jit(solution)/shard_map/ppermute | solution.py:236
  157.5 1.3 collective-permute-done.26.refs_0_
  158.8 9.8 %collective-permute-done.19 = bf16[8,48,512]{2,1,0:T(8,128)(2,1)S(1)} collective-permute-done((bf16[8,48,512]{2,1,0:T(8,128)(2,1)S(1)}, bf16[8,48,512]{2,1,0:T(8,128)(2,1)S(1)}, u32[]{:S(2)}, u32[]{:S(2)}) %collective-permute-start.19) | collective-permute-done | bytes 393248 | tf_op jit(solution)/shard_map/ppermute | solution.py:224
  168.6 2.5 %collective-permute-start.29 = (bf16[16,48,512]{2,1,0:T(8,128)(2,1)S(1)}, bf16[16,48,512]{2,1,0:T(8,128)(2,1)S(1)}, u32[]{:S(2)}, u32[]{:S(2)}) collective-permute-start(bf16[16,48,512]{2,1,0:T(8,128)(2,1)S(1)} %pad_maximum_fusion.1.refs_0_), channel_id=1, source_target_pairs={{0,8},{8,0},{1,9},{9,1},{2,10},{10,2},{3,11},{11,3},{4,12},{12,4},... | collective-permute-start | bytes 2359304 | tf_op jit(solution)/shard_map/ppermute | solution.py:236
  172.1 1.1 collective-permute-start.20
  173.1 1.7 place_0.5
  174.9 1.7 place_0.6
  176.6 1.7 place_0.7
  178.4 1.7 place_1.4
  180.1 1.7 place_1.5
  181.9 1.7 place_1.6
  184.7 1.9 %collective-permute-done.33.refs_1_ = bf16[16,48,512]{2,1,0:T(8,128)(2,1)S(1)} collective-permute-done((bf16[16,48,512]{2,1,0:T(8,128)(2,1)S(1)}, bf16[16,48,512]{2,1,0:T(8,128)(2,1)S(1)}, u32[]{:S(2)}, u32[]{:S(2)}) %collective-permute-start.33) | collective-permute-done | bytes 786464 | tf_op jit(solution)/shard_map/ppermute | solution.py:236
  186.6 2.3 %place_1.7 = (bf16[8,16,96,512]{3,2,1,0:T(8,128)(2,1)}, f32[8,128]{1,0:T(8,128)}) custom-call(s32[5]{0:T(128)S(1)} %stack.41.where.refs_0_, bf16[16,48,512]{2,1,0:T(8,128)(2,1)S(1)} %after.11.refs_0_, bf16[16,48,512]{2,1,0:T(8,128)(2,1)S(1)} %collective-permute-done.33.refs_1_, ...), custom_call_target="tpu_custom_call", output_to_operand_aliasing={{0}: (3, {})} | custom-call | tf_op jit(solution)/shard_map/place_1/pallas_call | solution.py:179
  (82 shorter events, 9.8 us)
Async XLA Ops:
  0.7 2.8 %copy-start = (bf16[2048,1536]{1,0:T(8,128)(2,1)S(1)}, bf16[2048,1536]{1,0:T(8,128)(2,1)}, u32[]{:S(2)}) copy-start(bf16[2048,1536]{1,0:T(8,128)(2,1)} %grads.1) | copy-start | bytes 18874372
  18.4 11.8 %collective-permute-start = (f16[384,4096]{1,0:T(8,128)(2,1)S(1)}, f16[384,4096]{1,0:T(8,128)(2,1)S(1)}, u32[]{:S(2)}, u32[]{:S(2)}) collective-permute-start(f16[384,4096]{1,0:T(8,128)(2,1)S(1)} %convolution_convert_fusion.1), channel_id=1, source_target_pairs={{0,8},{8,0},{1,9},{9,1},{2,10},{10,2},{3,11},{11,3},{4,12},{12,4},... | collective-permute-start | bytes 9437192 | tf_op jit(solution)/shard_map/ppermute | solution.py:268
  30.6 20.6 %collective-permute-start.1 = (f16[192,4096]{1,0:T(8,128)(2,1)S(1)}, f16[192,4096]{1,0:T(8,128)(2,1)S(1)}, u32[]{:S(2)}, u32[]{:S(2)}) collective-permute-start(f16[192,4096]{1,0:T(8,128)(2,1)S(1)} %fusion.1), channel_id=1, source_target_pairs={{0,32},{8,104},{32,0},{40,72},{64,96},{72,40},{96,64},{104,8},{1,3... | collective-permute-start | bytes 4718600 | tf_op jit(solution)/shard_map/ppermute | solution.py:224
  43.5 21.6 %collective-permute-start.2 = (f16[384,4096]{1,0:T(8,128)(2,1)S(1)}, f16[384,4096]{1,0:T(8,128)(2,1)S(1)}, u32[]{:S(2)}, u32[]{:S(2)}) collective-permute-start(f16[384,4096]{1,0:T(8,128)(2,1)S(1)} %convolution_convert_fusion), channel_id=1, source_target_pairs={{0,8},{8,0},{1,9},{9,1},{2,10},{10,2},{3,11},{11,3},{4,12},{12,4},... | collective-permute-start | bytes 9437192 | tf_op jit(solution)/shard_map/ppermute | solution.py:271
  51.4 11.4 %collective-permute-start.6 = (f16[96,4096]{1,0:T(8,128)(2,1)S(1)}, f16[96,4096]{1,0:T(8,128)(2,1)S(1)}, u32[]{:S(2)}, u32[]{:S(2)}) collective-permute-start(f16[96,4096]{1,0:T(8,128)(2,1)S(1)} %fusion.9), channel_id=1, source_target_pairs={{0,96},{8,40},{32,64},{40,8},{64,32},{72,104},{96,0},{104,72},{1,9... | collective-permute-start | bytes 2359304 | tf_op jit(solution)/shard_map/ppermute | solution.py:224
  63.3 9.2 %collective-permute-start.7 = (f16[48,4096]{1,0:T(8,128)(2,1)S(1)}, f16[48,4096]{1,0:T(8,128)(2,1)S(1)}, u32[]{:S(2)}, u32[]{:S(2)}) collective-permute-start(f16[48,4096]{1,0:T(8,128)(2,1)S(1)} %slice_convert_fusion), channel_id=1, source_target_pairs={{0,16},{16,0},{1,17},{17,1},{2,18},{18,2},{3,19},{19,3},{4,20},{20... | collective-permute-start | bytes 1179656 | tf_op jit(solution)/shard_map/ppermute | solution.py:262
  65.1 7.5 %copy-start.3 = (f32[1,96,4096]{2,1,0:T(8,128)S(1)}, f32[1,96,4096]{2,1,0:T(8,128)}, u32[]{:S(2)}) copy-start(f32[1,96,4096]{2,1,0:T(8,128)} %param.9) | copy-start | bytes 4718596
  65.5 20.6 %collective-permute-start.3 = (f16[192,4096]{1,0:T(8,128)(2,1)S(1)}, f16[192,4096]{1,0:T(8,128)(2,1)S(1)}, u32[]{:S(2)}, u32[]{:S(2)}) collective-permute-start(f16[192,4096]{1,0:T(8,128)(2,1)S(1)} %fusion), channel_id=1, source_target_pairs={{0,32},{8,104},{32,0},{40,72},{64,96},{72,40},{96,64},{104,8},{1,3... | collective-permute-start | bytes 4718600 | tf_op jit(solution)/shard_map/ppermute | solution.py:224
  68.1 4.5 %copy-start.1 = (f32[1,96,4096]{2,1,0:T(8,128)S(1)}, f32[1,96,4096]{2,1,0:T(8,128)}, u32[]{:S(2)}) copy-start(f32[1,96,4096]{2,1,0:T(8,128)} %param.7) | copy-start | bytes 4718596
  68.1 4.5 %copy-start.2 = (f32[1,96,4096]{2,1,0:T(8,128)S(1)}, f32[1,96,4096]{2,1,0:T(8,128)}, u32[]{:S(2)}) copy-start(f32[1,96,4096]{2,1,0:T(8,128)} %param.8) | copy-start | bytes 4718596
  75.5 6.3 %collective-permute-start.9 = (bf16[4,48,512]{2,1,0:T(8,128)(2,1)S(1)}, bf16[4,48,512]{2,1,0:T(8,128)(2,1)S(1)}, u32[]{:S(2)}, u32[]{:S(2)}) collective-permute-start(bf16[4,48,512]{2,1,0:T(8,128)(2,1)S(1)} %slice_bitcast_fusion), channel_id=1, source_target_pairs={{0,1},{1,0},{2,3},{3,2},{4,5},{5,4},{6,7},{7,6},{8,9},{9,8},{10,11... | collective-permute-start | bytes 589832 | tf_op jit(solution)/shard_map/ppermute | solution.py:121
  81.8 8.6 %collective-permute-start.10 = (bf16[2,48,512]{2,1,0:T(8,128)(2,1)S(1)}, bf16[2,48,512]{2,1,0:T(8,128)(2,1)S(1)}, u32[]{:S(2)}, u32[]{:S(2)}) collective-permute-start(bf16[2,48,512]{2,1,0:T(8,128)(2,1)S(1)} %pad_maximum_fusion.2), channel_id=1, source_target_pairs={{0,2},{2,4},{4,6},{6,0},{1,3},{3,5},{5,7},{7,1},{8,10},{10,12},{12... | collective-permute-start | bytes 294920 | tf_op jit(solution)/shard_map/ppermute | solution.py:123
  86.4 23.5 %collective-permute-start.4 = (f16[96,4096]{1,0:T(8,128)(2,1)S(1)}, f16[96,4096]{1,0:T(8,128)(2,1)S(1)}, u32[]{:S(2)}, u32[]{:S(2)}) collective-permute-start(f16[96,4096]{1,0:T(8,128)(2,1)S(1)} %fusion.5), channel_id=1, source_target_pairs={{0,96},{8,40},{32,64},{40,8},{64,32},{72,104},{96,0},{104,72},{1,9... | collective-permute-start | bytes 2359304 | tf_op jit(solution)/shard_map/ppermute | solution.py:224
  86.6 5.7 %collective-permute-start.11 = (bf16[2,48,512]{2,1,0:T(8,128)(2,1)S(1)}, bf16[2,48,512]{2,1,0:T(8,128)(2,1)S(1)}, u32[]{:S(2)}, u32[]{:S(2)}) collective-permute-start(bf16[2,48,512]{2,1,0:T(8,128)(2,1)S(1)} %pad_maximum_fusion.3), channel_id=1, source_target_pairs={{0,4},{2,6},{4,0},{6,2},{1,5},{3,7},{5,1},{7,3},{8,12},{10,14},{12... | collective-permute-start | bytes 294920 | tf_op jit(solution)/shard_map/ppermute | solution.py:123
  89.6 3.8 %collective-permute-start.12 = (bf16[2,48,512]{2,1,0:T(8,128)(2,1)S(1)}, bf16[2,48,512]{2,1,0:T(8,128)(2,1)S(1)}, u32[]{:S(2)}, u32[]{:S(2)}) collective-permute-start(bf16[2,48,512]{2,1,0:T(8,128)(2,1)S(1)} %pad_maximum_fusion.4), channel_id=1, source_target_pairs={{0,6},{2,0},{4,2},{6,4},{1,7},{3,1},{5,3},{7,5},{8,14},{10,8},{12,... | collective-permute-start | bytes 294920 | tf_op jit(solution)/shard_map/ppermute | solution.py:123
  94.6 6.9 %collective-permute-start.21 = (bf16[8,48,512]{2,1,0:T(8,128)(2,1)S(1)}, bf16[8,48,512]{2,1,0:T(8,128)(2,1)S(1)}, u32[]{:S(2)}, u32[]{:S(2)}) collective-permute-start(bf16[8,48,512]{2,1,0:T(8,128)(2,1)S(1)} %collect.2), channel_id=1, source_target_pairs={{0,96},{8,40},{32,64},{40,8},{64,32},{72,104},{96,0},{104,72},{1,9... | collective-permute-start | bytes 1179656 | tf_op jit(solution)/shard_map/ppermute | solution.py:224
  96.0 13.8 %collective-permute-start.13 = (bf16[8,48,512]{2,1,0:T(8,128)(2,1)S(1)}, bf16[8,48,512]{2,1,0:T(8,128)(2,1)S(1)}, u32[]{:S(2)}, u32[]{:S(2)}) collective-permute-start(bf16[8,48,512]{2,1,0:T(8,128)(2,1)S(1)} %collect.2), channel_id=1, source_target_pairs={{0,16},{16,0},{1,17},{17,1},{2,18},{18,2},{3,19},{19,3},{4,20},{20... | collective-permute-start | bytes 1179656 | tf_op jit(solution)/shard_map/ppermute | solution.py:228
  101.6 15.2 %collective-permute-start.22 = (bf16[16,48,512]{2,1,0:T(8,128)(2,1)S(1)}, bf16[16,48,512]{2,1,0:T(8,128)(2,1)S(1)}, u32[]{:S(2)}, u32[]{:S(2)}) collective-permute-start(bf16[16,48,512]{2,1,0:T(8,128)(2,1)S(1)} %pad_maximum_fusion.refs_0_), channel_id=1, source_target_pairs={{0,8},{8,0},{1,9},{9,1},{2,10},{10,2},{3,11},{11,3},{4,12},{12,4},... | collective-permute-start | bytes 2359304 | tf_op jit(solution)/shard_map/ppermute | solution.py:236
  109.8 6.9 %collective-permute-start.14 = (bf16[8,48,512]{2,1,0:T(8,128)(2,1)S(1)}, bf16[8,48,512]{2,1,0:T(8,128)(2,1)S(1)}, u32[]{:S(2)}, u32[]{:S(2)}) collective-permute-start(bf16[8,48,512]{2,1,0:T(8,128)(2,1)S(1)} %collective-permute-done.13), channel_id=1, source_target_pairs={{0,96},{8,40},{32,64},{40,8},{64,32},{72,104},{96,0},{104,72},{1,9... | collective-permute-start | bytes 1179656 | tf_op jit(solution)/shard_map/ppermute | solution.py:224
  110.3 8.8 %collective-permute-start.5 = (f16[48,4096]{1,0:T(8,128)(2,1)S(1)}, f16[48,4096]{1,0:T(8,128)(2,1)S(1)}, u32[]{:S(2)}, u32[]{:S(2)}) collective-permute-start(f16[48,4096]{1,0:T(8,128)(2,1)S(1)} %slice_convert_fusion.1), channel_id=1, source_target_pairs={{0,16},{16,0},{1,17},{17,1},{2,18},{18,2},{3,19},{19,3},{4,20},{20... | collective-permute-start | bytes 1179656 | tf_op jit(solution)/shard_map/ppermute | solution.py:262
  118.5 38.8 %collective-permute-start.23 = (bf16[16,48,512]{2,1,0:T(8,128)(2,1)S(1)}, bf16[16,48,512]{2,1,0:T(8,128)(2,1)S(1)}, u32[]{:S(2)}, u32[]{:S(2)}) collective-permute-start(bf16[16,48,512]{2,1,0:T(8,128)(2,1)S(1)} %after.10), channel_id=1, source_target_pairs={{0,32},{8,104},{32,0},{40,72},{64,96},{72,40},{96,64},{104,8},{1,3... | collective-permute-start | bytes 2359304 | tf_op jit(solution)/shard_map/ppermute | solution.py:224
  122.1 6.4 %collective-permute-start.8 = (bf16[4,48,512]{2,1,0:T(8,128)(2,1)S(1)}, bf16[4,48,512]{2,1,0:T(8,128)(2,1)S(1)}, u32[]{:S(2)}, u32[]{:S(2)}) collective-permute-start(bf16[4,48,512]{2,1,0:T(8,128)(2,1)S(1)} %slice_bitcast_fusion.1), channel_id=1, source_target_pairs={{0,1},{1,0},{2,3},{3,2},{4,5},{5,4},{6,7},{7,6},{8,9},{9,8},{10,11... | collective-permute-start | bytes 589832 | tf_op jit(solution)/shard_map/ppermute | solution.py:121
  128.6 4.7 %collective-permute-start.15 = (bf16[2,48,512]{2,1,0:T(8,128)(2,1)S(1)}, bf16[2,48,512]{2,1,0:T(8,128)(2,1)S(1)}, u32[]{:S(2)}, u32[]{:S(2)}) collective-permute-start(bf16[2,48,512]{2,1,0:T(8,128)(2,1)S(1)} %pad_maximum_fusion.5), channel_id=1, source_target_pairs={{0,2},{2,4},{4,6},{6,0},{1,3},{3,5},{5,7},{7,1},{8,10},{10,12},{12... | collective-permute-start | bytes 294920 | tf_op jit(solution)/shard_map/ppermute | solution.py:123
  128.9 5.7 %collective-permute-start.16 = (bf16[2,48,512]{2,1,0:T(8,128)(2,1)S(1)}, bf16[2,48,512]{2,1,0:T(8,128)(2,1)S(1)}, u32[]{:S(2)}, u32[]{:S(2)}) collective-permute-start(bf16[2,48,512]{2,1,0:T(8,128)(2,1)S(1)} %pad_maximum_fusion.6), channel_id=1, source_target_pairs={{0,4},{2,6},{4,0},{6,2},{1,5},{3,7},{5,1},{7,3},{8,12},{10,14},{12... | collective-permute-start | bytes 294920 | tf_op jit(solution)/shard_map/ppermute | solution.py:123
  131.6 3.5 %collective-permute-start.17 = (bf16[2,48,512]{2,1,0:T(8,128)(2,1)S(1)}, bf16[2,48,512]{2,1,0:T(8,128)(2,1)S(1)}, u32[]{:S(2)}, u32[]{:S(2)}) collective-permute-start(bf16[2,48,512]{2,1,0:T(8,128)(2,1)S(1)} %pad_maximum_fusion.7), channel_id=1, source_target_pairs={{0,6},{2,0},{4,2},{6,4},{1,7},{3,1},{5,3},{7,5},{8,14},{10,8},{12,... | collective-permute-start | bytes 294920 | tf_op jit(solution)/shard_map/ppermute | solution.py:123
  136.3 14.0 %collective-permute-start.28 = (bf16[8,48,512]{2,1,0:T(8,128)(2,1)S(1)}, bf16[8,48,512]{2,1,0:T(8,128)(2,1)S(1)}, u32[]{:S(2)}, u32[]{:S(2)}) collective-permute-start(bf16[8,48,512]{2,1,0:T(8,128)(2,1)S(1)} %collect.3), channel_id=1, source_target_pairs={{0,96},{8,40},{32,64},{40,8},{64,32},{72,104},{96,0},{104,72},{1,9... | collective-permute-start | bytes 1179656 | tf_op jit(solution)/shard_map/ppermute | solution.py:224
  143.2 15.6 %collective-permute-start.26 = (bf16[16,48,512]{2,1,0:T(8,128)(2,1)S(1)}, bf16[16,48,512]{2,1,0:T(8,128)(2,1)S(1)}, u32[]{:S(2)}, u32[]{:S(2)}) collective-permute-start(bf16[16,48,512]{2,1,0:T(8,128)(2,1)S(1)} %constant_dynamic-update-slice_fusion.refs_1_.refs_0_), channel_id=1, source_target_pairs={{0,32},{8,104},{32,0},{40,72},{64,96},{72,40},{96,64},{104,8},{1,3... | collective-permute-start | bytes 2359304 | tf_op jit(solution)/shard_map/ppermute | solution.py:224
  143.2 14.2 %collective-permute-start.18 = (bf16[8,48,512]{2,1,0:T(8,128)(2,1)S(1)}, bf16[8,48,512]{2,1,0:T(8,128)(2,1)S(1)}, u32[]{:S(2)}, u32[]{:S(2)}) collective-permute-start(bf16[8,48,512]{2,1,0:T(8,128)(2,1)S(1)} %collect.3), channel_id=1, source_target_pairs={{0,16},{16,0},{1,17},{17,1},{2,18},{18,2},{3,19},{19,3},{4,20},{20... | collective-permute-start | bytes 1179656 | tf_op jit(solution)/shard_map/ppermute | solution.py:228
  150.4 21.0 %collective-permute-start.30 = (bf16[16,48,512]{2,1,0:T(8,128)(2,1)S(1)}, bf16[16,48,512]{2,1,0:T(8,128)(2,1)S(1)}, u32[]{:S(2)}, u32[]{:S(2)}) collective-permute-start(bf16[16,48,512]{2,1,0:T(8,128)(2,1)S(1)} %pad_maximum_fusion.1.refs_0_), channel_id=1, source_target_pairs={{0,32},{8,104},{32,0},{40,72},{64,96},{72,40},{96,64},{104,8},{1,3... | collective-permute-start | bytes 2359304 | tf_op jit(solution)/shard_map/ppermute | solution.py:224
  150.5 21.0 %collective-permute-start.25 = (bf16[16,48,512]{2,1,0:T(8,128)(2,1)S(1)}, bf16[16,48,512]{2,1,0:T(8,128)(2,1)S(1)}, u32[]{:S(2)}, u32[]{:S(2)}) collective-permute-start(bf16[16,48,512]{2,1,0:T(8,128)(2,1)S(1)} %constant_dynamic-update-slice_fusion.refs_1_.refs_0_), channel_id=1, source_target_pairs={{0,8},{8,0},{1,9},{9,1},{2,10},{10,2},{3,11},{11,3},{4,12},{12,4},... | collective-permute-start | bytes 2359304 | tf_op jit(solution)/shard_map/ppermute | solution.py:236
  157.3 14.7 %collective-permute-start.24 = (bf16[16,48,512]{2,1,0:T(8,128)(2,1)S(1)}, bf16[16,48,512]{2,1,0:T(8,128)(2,1)S(1)}, u32[]{:S(2)}, u32[]{:S(2)}) collective-permute-start(bf16[16,48,512]{2,1,0:T(8,128)(2,1)S(1)} %collective-permute-done.23.refs_0_), channel_id=1, source_target_pairs={{0,8},{8,0},{1,9},{9,1},{2,10},{10,2},{3,11},{11,3},{4,12},{12,4},... | collective-permute-start | bytes 2359304 | tf_op jit(solution)/shard_map/ppermute | solution.py:236
  157.4 11.3 %collective-permute-start.19 = (bf16[8,48,512]{2,1,0:T(8,128)(2,1)S(1)}, bf16[8,48,512]{2,1,0:T(8,128)(2,1)S(1)}, u32[]{:S(2)}, u32[]{:S(2)}) collective-permute-start(bf16[8,48,512]{2,1,0:T(8,128)(2,1)S(1)} %collective-permute-done.18), channel_id=1, source_target_pairs={{0,96},{8,40},{32,64},{40,8},{64,32},{72,104},{96,0},{104,72},{1,9... | collective-permute-start | bytes 1179656 | tf_op jit(solution)/shard_map/ppermute | solution.py:224
  158.8 17.8 %collective-permute-start.27 = (bf16[16,48,512]{2,1,0:T(8,128)(2,1)S(1)}, bf16[16,48,512]{2,1,0:T(8,128)(2,1)S(1)}, u32[]{:S(2)}, u32[]{:S(2)}) collective-permute-start(bf16[16,48,512]{2,1,0:T(8,128)(2,1)S(1)} %collective-permute-done.26.refs_0_), channel_id=1, source_target_pairs={{0,8},{8,0},{1,9},{9,1},{2,10},{10,2},{3,11},{11,3},{4,12},{12,4},... | collective-permute-start | bytes 2359304 | tf_op jit(solution)/shard_map/ppermute | solution.py:236
  168.6 9.7 %collective-permute-start.29 = (bf16[16,48,512]{2,1,0:T(8,128)(2,1)S(1)}, bf16[16,48,512]{2,1,0:T(8,128)(2,1)S(1)}, u32[]{:S(2)}, u32[]{:S(2)}) collective-permute-start(bf16[16,48,512]{2,1,0:T(8,128)(2,1)S(1)} %pad_maximum_fusion.1.refs_0_), channel_id=1, source_target_pairs={{0,8},{8,0},{1,9},{9,1},{2,10},{10,2},{3,11},{11,3},{4,12},{12,4},... | collective-permute-start | bytes 2359304 | tf_op jit(solution)/shard_map/ppermute | solution.py:236
  171.5 8.6 %collective-permute-start.31 = (bf16[16,48,512]{2,1,0:T(8,128)(2,1)S(1)}, bf16[16,48,512]{2,1,0:T(8,128)(2,1)S(1)}, u32[]{:S(2)}, u32[]{:S(2)}) collective-permute-start(bf16[16,48,512]{2,1,0:T(8,128)(2,1)S(1)} %collective-permute-done.30.refs_0_), channel_id=1, source_target_pairs={{0,8},{8,0},{1,9},{9,1},{2,10},{10,2},{3,11},{11,3},{4,12},{12,4},... | collective-permute-start | bytes 2359304 | tf_op jit(solution)/shard_map/ppermute | solution.py:236
  171.6 10.3 %collective-permute-start.32 = (bf16[16,48,512]{2,1,0:T(8,128)(2,1)S(1)}, bf16[16,48,512]{2,1,0:T(8,128)(2,1)S(1)}, u32[]{:S(2)}, u32[]{:S(2)}) collective-permute-start(bf16[16,48,512]{2,1,0:T(8,128)(2,1)S(1)} %constant_dynamic-update-slice_fusion.2.refs_0_), channel_id=1, source_target_pairs={{0,8},{8,0},{1,9},{9,1},{2,10},{10,2},{3,11},{11,3},{4,12},{12,4},... | collective-permute-start | bytes 2359304 | tf_op jit(solution)/shard_map/ppermute | solution.py:236
  172.1 12.1 %collective-permute-start.20 = (bf16[16,48,512]{2,1,0:T(8,128)(2,1)S(1)}, bf16[16,48,512]{2,1,0:T(8,128)(2,1)S(1)}, u32[]{:S(2)}, u32[]{:S(2)}) collective-permute-start(bf16[16,48,512]{2,1,0:T(8,128)(2,1)S(1)} %constant_dynamic-update-slice_fusion.2.refs_0_), channel_id=1, source_target_pairs={{0,32},{8,104},{32,0},{40,72},{64,96},{72,40},{96,64},{104,8},{1,3... | collective-permute-start | bytes 2359304 | tf_op jit(solution)/shard_map/ppermute | solution.py:224
  184.1 2.5 %collective-permute-start.33 = (bf16[16,48,512]{2,1,0:T(8,128)(2,1)S(1)}, bf16[16,48,512]{2,1,0:T(8,128)(2,1)S(1)}, u32[]{:S(2)}, u32[]{:S(2)}) collective-permute-start(bf16[16,48,512]{2,1,0:T(8,128)(2,1)S(1)} %after.11.refs_0_), channel_id=1, source_target_pairs={{0,8},{8,0},{1,9},{9,1},{2,10},{10,2},{3,11},{11,3},{4,12},{12,4},... | collective-permute-start | bytes 2359304 | tf_op jit(solution)/shard_map/ppermute | solution.py:236
where the time goes:
time: 189 us
  waiting for transfers between devices  60.4 us (32%)
  starting transfers between devices  53.6 us (28%)
  matrix products  41.1 us (22%)
  Pallas kernels  27 us (14%)
  local copies, waits for them, and re-layouts  3.06 us (2%)
  other arithmetic  2.68 us (1%)
    ppermute x12, waiting for transfers between devices, swap(): return lax.ppermute(a, ('x', 'c'), SWAPS[k])  41.7 us
    dot_general x4, matrix products, dot(): return jnp.dot(a, b, preferred_element_type=F32)  41.1 us
    ppermute x8, starting transfers between devices, gather(): lax.ppermute(a, 'c', SWAP)  18.7 us
    ppermute x12, starting transfers between devices, swap(): return lax.ppermute(a, ('x', 'c'), SWAPS[k])  15.9 us
    pallas_call x8, Pallas kernels, place(): pl.pallas_call(kernel, grid_spec=pltpu.PrefetchScalarGridSpec(num_scalar_...  14.4 us
    ppermute x6, starting transfers between devices, exchange(): lax.ppermute(jnp.stack([rounded[0, k], got[k]]), 'y', [(i, (i + k) % 4) f...  8.83 us
    ppermute x2, starting transfers between devices, exchange(): got = after(lax.ppermute(rounded[1], 'zh', SWAP), *gate)  6.62 us
    ppermute x2, waiting for transfers between devices, exchange(): got = after(lax.ppermute(rounded[1], 'zh', SWAP), *gate)  6.09 us
  transfers between devices with their start and end apart: 34, of which 20 were waited for; matrix products, arithmetic and copies ran while one was open for 18% of the time, Pallas kernels for 11%

commit v1 on v0

--- a/solution.py
+++ b/solution.py
@@ -38,16 +38,13 @@
             owner, at = row // 96, row % 96
             piece = turned[16 * q : 16 * q + 16]
             same = jnp.where(z == owner // 2, 1, 0)
-            start = 0
-            for k, count in enumerate(CHUNKS):
+            for k, (start, count) in enumerate(zip(STARTS, CHUNKS)):
                 if start <= at < start + count:
                     for keep in range(2):
 
                         @pl.when((c == owner % 2) == (keep == 1))
                         def _():
                             outs[2 * k + keep][0, same, at - start : at - start + 16, :] = piece
-
-                start += count
 
 
 def order_rows(where, logit_grads):
@@ -150,8 +147,8 @@
     )(where, rounded, got, *came)
 
 
-def place(where, arrays, pieces, head, group):
-    given = () if head is None else (head,)
+def place(where, arrays, pieces, head, group, others=()):
+    given = (*others, *(() if head is None else (head,)))
 
     def kernel(where, *refs):
         out, mark, sem = refs[-3:]
@@ -186,7 +183,7 @@
             scratch_shapes=[pltpu.SemaphoreType.DMA((len(pieces),))],
         ),
         out_shape=[jax.ShapeDtypeStruct((8, 16, 96, 512), BF16), jax.ShapeDtypeStruct((8, 128), F32)],
-        input_output_aliases={} if head is None else {1 + len(arrays): 0},
+        input_output_aliases={} if head is None else {len(arrays) + len(given): 0},
         compiler_params=params(1),
         name=f"place_{group}",
     )(where, *arrays, *given)
@@ -224,18 +221,22 @@
     return lax.ppermute(a, ("x", "c"), SWAPS[k])
 
 
-def gather(where, mine, head, group, marks, gate):
+def gather(mine, gate):
     side = lax.ppermute(mine, "zl", SWAP)
+    pairs, fars = [], []
     for z, own in enumerate((mine, side)):
-        pair = jnp.concatenate([own, swap(own, 1)], 0)
-        far = swap(after(pair, *gate) if z == 0 else pair, 0)
-        for at, a in ((0, pair), (2, far)):
-            if group == 1 and z == 1 and at == 2:
-                a = after(a, *marks)
-            pieces = [(c, 8 * k, (at + k, z, c)) for c in range(2) for k in range(2)]
-            head, mark = place(where, (a, lax.ppermute(a, "c", SWAP)), pieces, head, group)
-            marks = marks + [mark]
-    return head, marks, pair
+        pairs.append(jnp.concatenate([own, swap(own, 1)], 0))
+        fars.append(swap(after(pairs[z], *gate) if z == 0 else pairs[z], 0))
+    return pairs, fars
+
+
+def place_all(where, chains, head, group, others=()):
+    arrays, pieces = [], []
+    for a, at, z in chains:
+        for c, source in enumerate((a, lax.ppermute(a, "c", SWAP))):
+            pieces += [(len(arrays), 8 * k, (at + k, z, c)) for k in range(2)]
+            arrays.append(source)
+    return place(where, arrays, pieces, head, group, others)
 
 
 def local(hidden_states, logit_grads, master, moment_one, moment_two):
@@ -252,7 +253,7 @@
         n = keep.shape[0] // 4
         total = keep[2 * n : 3 * n] + wide(came[2 * n : 3 * n]) + wide(got[:n])
         if after_this is not None:
-            total = total + after_this.reshape(-1)[:1].astype(F32)[:, None] * 0
+            total = total + after_this.astype(F32) * 0
         sent = total.astype(F16)
         return swap(sent, 1), sent
 
@@ -263,7 +264,7 @@
 
     def update(gradient, outs, group, gate):
         outs, rounded = adam(where, gradient, (master[0], moment_one[0], moment_two[0]), outs, group)
-        return outs, exchange(where, rounded, gate)
+        return outs, exchange(where, rounded, gate), rounded[0, 0, :1, :1]
 
     came_a = lax.ppermute(dot(rows[0], hidden_states).astype(F16), "c", SWAP)
     keep_a = dot(rows[1], hidden_states)
@@ -273,12 +274,16 @@
     keep_b = dot(after(rows[3], sent), hidden_states)
     first_b, sent = send_first(keep_b, came_b)
     gradient, _ = send_side(keep_a, came_a, first_a, second_a)
-    outs, mine = update(after(gradient, sent), None, 0, ())
-    second_b, _ = send_second(keep_b, came_b, first_b, None)
+    outs, mine, done = update(after(gradient, sent), None, 0, ())
+    second_b, _ = send_second(keep_b, came_b, first_b, done)
     gradient, own = send_side(keep_b, came_b, first_b, second_b)
-    head, marks, pair = gather(where, mine, None, 0, [], (own,))
-    outs, mine = update(gradient, outs, 1, (pair,))
-    head, _, _ = gather(where, mine, head, 1, marks, ())
+    pairs_a, fars_a = gather(after(mine, own), ())
+    outs, mine, _ = update(after(gradient, pairs_a[0]), outs, 1, (pairs_a[1],))
+    pairs_b, fars_b = gather(after(mine, fars_a[0]), (fars_a[1],))
+    chains = [(a, at, z) for z in range(2) for a, at in ((pairs_a[z], 0), (fars_a[z], 2))]
+    head, _ = place_all(where, chains, None, 0, (pairs_b[1],))
+    head, mark = place_all(where, [(pairs_b[0], 0, 0), (fars_b[0], 2, 0), (pairs_b[1], 0, 1)], head, 1)
+    head, _ = place_all(where, [(after(fars_b[1], mark), 2, 1)], head, 1)
     return (*(o[None] for o in outs), head.reshape(12288, 512))
 
 

time: 189 us -> 185 us (0.979)
  Pallas kernels: 27 us -> 21.7 us
  starting transfers between devices: 53.6 us -> 48.7 us
  waiting for transfers between devices: 60.4 us -> 64.8 us
    ppermute x8, starting transfers between devices: 18.7 us -> 6.11 us  [place_all(): lax.ppermute(a, 'c', SWAP)]
    ppermute x12, starting transfers between devices: 15.9 us -> 22.8 us  [swap(): return lax.ppermute(a, ('x', 'c'), SWAPS[k])]
    ppermute x2, waiting for transfers between devices: 6.09 us -> 0.01 us  [exchange(): got = after(lax.ppermute(rounded[1], 'zh', SWAP), *gate)]
    ppermute x6, waiting for transfers between devices: 5.95 us -> 12 us  [exchange(): lax.ppermute(jnp.stack([rounded[0, k], got[k]]), 'y', [(i, (i + k) % 4) f...]
    pallas_call x8 -> x3, Pallas kernels: 14.4 us -> 9.06 us  [place(): pl.pallas_call(kernel, grid_spec=pltpu.PrefetchScalarGridSpec(num_scalar_...]
  transfers between devices with their start and end apart: 34 -> 34, of which waited for: 20 -> 19; matrix products, arithmetic and copies ran while one was open for 18% -> 18% of each run, Pallas kernels for 11% -> 8%
where the time goes in v1:
time: 185 us
  waiting for transfers between devices  64.8 us (35%)
  starting transfers between devices  48.7 us (26%)
  matrix products  41.1 us (22%)
  Pallas kernels  21.7 us (12%)
  local copies, waits for them, and re-layouts  3.62 us (2%)
  other arithmetic  2.78 us (2%)
  between operations  1.87 us (1%)
    ppermute x12, waiting for transfers between devices, swap(): return lax.ppermute(a, ('x', 'c'), SWAPS[k])  43.6 us
    dot_general x4, matrix products, dot(): return jnp.dot(a, b, preferred_element_type=F32)  41.1 us
    ppermute x12, starting transfers between devices, swap(): return lax.ppermute(a, ('x', 'c'), SWAPS[k])  22.8 us
    ppermute x6, waiting for transfers between devices, exchange(): lax.ppermute(jnp.stack([rounded[0, k], got[k]]), 'y', [(i, (i + k) % 4) f...  12 us
    pallas_call x3, Pallas kernels, place(): pl.pallas_call(kernel, grid_spec=pltpu.PrefetchScalarGridSpec(num_scalar_...  9.06 us
    ppermute x6, starting transfers between devices, exchange(): lax.ppermute(jnp.stack([rounded[0, k], got[k]]), 'y', [(i, (i + k) % 4) f...  7.86 us
    ppermute x2, starting transfers between devices, exchange(): got = after(lax.ppermute(rounded[1], 'zh', SWAP), *gate)  6.63 us
    ppermute x8, starting transfers between devices, place_all(): lax.ppermute(a, 'c', SWAP)  6.11 us
  transfers between devices with their start and end apart: 34, of which 19 were waited for; matrix products, arithmetic and copies ran while one was open for 18% of the time, Pallas kernels for 8%

profile of v1, /device:TPU:1, one launch (start us, length us, event | category | flops | bytes accessed | tf_op | source)
XLA Modules:
  0.0 184.5 jit_solution(6028967042842478289)
XLA Ops:
  0.7 2.8 %copy-done = bf16[2048,1536]{1,0:T(8,128)(2,1)S(1)} copy-done((bf16[2048,1536]{1,0:T(8,128)(2,1)S(1)}, bf16[2048,1536]{1,0:T(8,128)(2,1)}, u32[]{:S(2)}) %copy-start) | copy-done | bytes 6291480
  3.5 4.5 %order_rows.1 = (bf16[4,2,48,2048]{3,2,1,0:T(8,128)(2,1)S(1)}, bf16[4,2,48,2048]{3,2,1,0:T(8,128)(2,1)S(1)}, bf16[4,2,48,2048]{3,2,1,0:T(8,128)(2,1)S(1)}, bf16[4,2,48,2048]{3,2,1,0:T(8,128)(2,1)S(1)}) custom-call(s32[5]{0:T(128)S(1)} %stack.41.where.refs_0_, bf16[2048,1536]{1,0:T(8,128)(2,1)S(1)} %copy-done), custom_call_target="tpu_custom_call" | custom-call | tf_op jit(solution)/shard_map/order_rows/pallas_call | solution.py:58
  8.1 10.3 %convolution_convert_fusion.1 = f16[384,4096]{1,0:T(8,128)(2,1)S(1)} fusion(bf16[384,2048]{1,0:T(8,128)(2,1)S(1)} %bitcast.50, bf16[2048,4096]{1,0:T(8,128)(2,1)} %param.5), kind=kOutput, calls=%fused_computation.1 | convolution fusion | flops 6444023808 | bytes 21495808 | tf_op jit(solution)/shard_map/dot_general | solution.py:217
  18.4 1.5 collective-permute-start
  19.8 10.3 %fusion.13.refs_1_ = f32[384,4096]{1,0:T(8,128)S(1)} fusion(bf16[384,2048]{1,0:T(8,128)(2,1)S(1)} %bitcast.49, bf16[2048,4096]{1,0:T(8,128)(2,1)} %param.5), kind=kOutput, calls=%fused_computation.47 | convolution fusion | flops 6442450944 | bytes 24641536 | tf_op jit(solution)/shard_map/dot_general | solution.py:217
  30.6 2.6 %collective-permute-start.1 = (f16[192,4096]{1,0:T(8,128)(2,1)S(1)}, f16[192,4096]{1,0:T(8,128)(2,1)S(1)}, u32[]{:S(2)}, u32[]{:S(2)}) collective-permute-start(f16[192,4096]{1,0:T(8,128)(2,1)S(1)} %fusion.1), channel_id=1, source_target_pairs={{0,32},{8,104},{32,0},{40,72},{64,96},{72,40},{96,64},{104,8},{1,3... | collective-permute-start | bytes 4718600 | tf_op jit(solution)/shard_map/ppermute | solution.py:221
  33.2 10.3 %convolution_convert_fusion = f16[384,4096]{1,0:T(8,128)(2,1)S(1)} fusion(bf16[384,2048]{1,0:T(8,128)(2,1)S(1)} %after.10, bf16[2048,4096]{1,0:T(8,128)(2,1)} %param.5), kind=kOutput, calls=%fused_computation | convolution fusion | flops 6444023808 | bytes 21495808 | tf_op jit(solution)/shard_map/dot_general | solution.py:217
  43.6 7.5 %collective-permute-done.1 = f16[192,4096]{1,0:T(8,128)(2,1)S(1)} collective-permute-done((f16[192,4096]{1,0:T(8,128)(2,1)S(1)}, f16[192,4096]{1,0:T(8,128)(2,1)S(1)}, u32[]{:S(2)}, u32[]{:S(2)}) %collective-permute-start.1) | collective-permute-done | bytes 1572896 | tf_op jit(solution)/shard_map/ppermute | solution.py:221
  51.4 0.6 collective-permute-start.4
  52.1 10.3 %fusion.14 = f32[384,4096]{1,0:T(8,128)S(1)} fusion(bf16[384,2048]{1,0:T(8,128)(2,1)S(1)} %after.9, bf16[2048,4096]{1,0:T(8,128)(2,1)} %param.5), kind=kOutput, calls=%fused_computation.48 | convolution fusion | flops 6442450944 | bytes 24641536 | tf_op jit(solution)/shard_map/dot_general | solution.py:217
  63.3 1.8 collective-permute-start.5
  65.5 2.6 %collective-permute-start.3 = (f16[192,4096]{1,0:T(8,128)(2,1)S(1)}, f16[192,4096]{1,0:T(8,128)(2,1)S(1)}, u32[]{:S(2)}, u32[]{:S(2)}) collective-permute-start(f16[192,4096]{1,0:T(8,128)(2,1)S(1)} %fusion), channel_id=1, source_target_pairs={{0,32},{8,104},{32,0},{40,72},{64,96},{72,40},{96,64},{104,8},{1,3... | collective-permute-start | bytes 4718600 | tf_op jit(solution)/shard_map/ppermute | solution.py:221
  68.1 4.4 %collective-permute-done.5 = f16[48,4096]{1,0:T(8,128)(2,1)S(1)} collective-permute-done((f16[48,4096]{1,0:T(8,128)(2,1)S(1)}, f16[48,4096]{1,0:T(8,128)(2,1)S(1)}, u32[]{:S(2)}, u32[]{:S(2)}) %collective-permute-start.5) | collective-permute-done | bytes 393248 | tf_op jit(solution)/shard_map/ppermute | solution.py:263
  72.6 2.9 %adam_0.1 = (f32[96,4096]{1,0:T(8,128)}, f32[96,4096]{1,0:T(8,128)}, f32[96,4096]{1,0:T(8,128)}, bf16[2,4,48,512]{3,2,1,0:T(8,128)(2,1)S(1)}) custom-call(s32[5]{0:T(128)S(1)} %stack.41.where.refs_0_, f32[48,4096]{1,0:T(8,128)S(1)} %after.11.refs_1_, f32[96,4096]{1,0:T(8,128)S(1)} %bitcast.41, f32[96,4096]{1,0:T(8,128)S(1)} %bitcast.43, f32[96,4096]{1,0:T(8,128)S(1)} %bitcast.45), custom_call_target="tpu_custom_call" | custom-call | tf_op jit(solution)/shard_map/adam_0/pallas_call | solution.py:99
  76.0 3.2 %collective-permute-start.8 = (bf16[4,48,512]{2,1,0:T(8,128)(2,1)S(1)}, bf16[4,48,512]{2,1,0:T(8,128)(2,1)S(1)}, u32[]{:S(2)}, u32[]{:S(2)}) collective-permute-start(bf16[4,48,512]{2,1,0:T(8,128)(2,1)S(1)} %slice_bitcast_fusion.1), channel_id=1, source_target_pairs={{0,1},{1,0},{2,3},{3,2},{4,5},{5,4},{6,7},{7,6},{8,9},{9,8},{10,11... | collective-permute-start | bytes 589832 | tf_op jit(solution)/shard_map/ppermute | solution.py:118
  79.9 6.2 %collective-permute-done.3 = f16[192,4096]{1,0:T(8,128)(2,1)S(1)} collective-permute-done((f16[192,4096]{1,0:T(8,128)(2,1)S(1)}, f16[192,4096]{1,0:T(8,128)(2,1)S(1)}, u32[]{:S(2)}, u32[]{:S(2)}) %collective-permute-start.3) | collective-permute-done | bytes 1572896 | tf_op jit(solution)/shard_map/ppermute | solution.py:221
  86.7 2.8 %collective-permute-start.11 = (bf16[2,48,512]{2,1,0:T(8,128)(2,1)S(1)}, bf16[2,48,512]{2,1,0:T(8,128)(2,1)S(1)}, u32[]{:S(2)}, u32[]{:S(2)}) collective-permute-start(bf16[2,48,512]{2,1,0:T(8,128)(2,1)S(1)} %pad_maximum_fusion.4), channel_id=1, source_target_pairs={{0,6},{2,0},{4,2},{6,4},{1,7},{3,1},{5,3},{7,5},{8,14},{10,8},{12,... | collective-permute-start | bytes 294920 | tf_op jit(solution)/shard_map/ppermute | solution.py:120
  90.0 0.8 collective-permute-start.9
  91.1 3.5 %collective-permute-done.10.two = bf16[2,48,512]{2,1,0:T(8,128)(2,1)S(1)} collective-permute-done((bf16[2,48,512]{2,1,0:T(8,128)(2,1)S(1)}, bf16[2,48,512]{2,1,0:T(8,128)(2,1)S(1)}, u32[]{:S(2)}, u32[]{:S(2)}) %collective-permute-start.10) | collective-permute-done | bytes 98336 | tf_op jit(solution)/shard_map/ppermute | solution.py:120
  94.7 1.2 collective-permute-done.9.one
  95.9 1.2 collect.2.refs_0_
  98.9 1.3 collective-permute-start.14
  100.2 4.5 %collective-permute-done.12 = bf16[8,48,512]{2,1,0:T(8,128)(2,1)S(1)} collective-permute-done((bf16[8,48,512]{2,1,0:T(8,128)(2,1)S(1)}, bf16[8,48,512]{2,1,0:T(8,128)(2,1)S(1)}, u32[]{:S(2)}, u32[]{:S(2)}) %collective-permute-start.12) | collective-permute-done | bytes 393248 | tf_op jit(solution)/shard_map/ppermute | solution.py:221
  104.8 3.3 %collective-permute-start.19 = (bf16[16,48,512]{2,1,0:T(8,128)(2,1)S(1)}, bf16[16,48,512]{2,1,0:T(8,128)(2,1)S(1)}, u32[]{:S(2)}, u32[]{:S(2)}) collective-permute-start(bf16[16,48,512]{2,1,0:T(8,128)(2,1)S(1)} %pad_maximum_fusion.refs_1_.refs_0_), channel_id=1, source_target_pairs={{0,32},{8,104},{32,0},{40,72},{64,96},{72,40},{96,64},{104,8},{1,3... | collective-permute-start | bytes 2359304 | tf_op jit(solution)/shard_map/ppermute | solution.py:221
  108.3 2.9 %adam_1.1 = (f32[96,4096]{1,0:T(8,128)}, f32[96,4096]{1,0:T(8,128)}, f32[96,4096]{1,0:T(8,128)}, bf16[2,4,48,512]{3,2,1,0:T(8,128)(2,1)S(1)}) custom-call(s32[5]{0:T(128)S(1)} %stack.41.where.refs_0_, f32[48,4096]{1,0:T(8,128)S(1)} %after.13.refs_1_, f32[96,4096]{1,0:T(8,128)S(1)} %bitcast.42, ...), custom_call_target="tpu_custom_call", output_to_operand_aliasing={{0}: (5, {}), {1}: (6, {}), {2}: (7, {})} | custom-call | tf_op jit(solution)/shard_map/adam_1/pallas_call | solution.py:99
  111.2 3.6 %collective-permute-start.15 = (bf16[8,48,512]{2,1,0:T(8,128)(2,1)S(1)}, bf16[8,48,512]{2,1,0:T(8,128)(2,1)S(1)}, u32[]{:S(2)}, u32[]{:S(2)}) collective-permute-start(bf16[8,48,512]{2,1,0:T(8,128)(2,1)S(1)} %collective-permute-done.14), channel_id=1, source_target_pairs={{0,96},{8,40},{32,64},{40,8},{64,32},{72,104},{96,0},{104,72},{1,9... | collective-permute-start | bytes 1179656 | tf_op jit(solution)/shard_map/ppermute | solution.py:221
  114.8 3.4 %collective-permute-start.13 = (bf16[4,48,512]{2,1,0:T(8,128)(2,1)S(1)}, bf16[4,48,512]{2,1,0:T(8,128)(2,1)S(1)}, u32[]{:S(2)}, u32[]{:S(2)}) collective-permute-start(bf16[4,48,512]{2,1,0:T(8,128)(2,1)S(1)} %slice_bitcast_fusion), channel_id=1, source_target_pairs={{0,1},{1,0},{2,3},{3,2},{4,5},{5,4},{6,7},{7,6},{8,9},{9,8},{10,11... | collective-permute-start | bytes 589832 | tf_op jit(solution)/shard_map/ppermute | solution.py:118
  118.2 4.7 %collective-permute-done.15 = bf16[8,48,512]{2,1,0:T(8,128)(2,1)S(1)} collective-permute-done((bf16[8,48,512]{2,1,0:T(8,128)(2,1)S(1)}, bf16[8,48,512]{2,1,0:T(8,128)(2,1)S(1)}, u32[]{:S(2)}, u32[]{:S(2)}) %collective-permute-start.15) | collective-permute-done | bytes 393248 | tf_op jit(solution)/shard_map/ppermute | solution.py:221
  122.9 6.8 %collective-permute-start.25 = (bf16[16,48,512]{2,1,0:T(8,128)(2,1)S(1)}, bf16[16,48,512]{2,1,0:T(8,128)(2,1)S(1)}, u32[]{:S(2)}, u32[]{:S(2)}) collective-permute-start(bf16[16,48,512]{2,1,0:T(8,128)(2,1)S(1)} %constant_dynamic-update-slice_fusion.refs_1_.refs_4_), channel_id=1, source_target_pairs={{0,32},{8,104},{32,0},{40,72},{64,96},{72,40},{96,64},{104,8},{1,3... | collective-permute-start | bytes 2359304 | tf_op jit(solution)/shard_map/ppermute | solution.py:221
  129.7 2.7 %collective-permute-start.18 = (bf16[2,48,512]{2,1,0:T(8,128)(2,1)S(1)}, bf16[2,48,512]{2,1,0:T(8,128)(2,1)S(1)}, u32[]{:S(2)}, u32[]{:S(2)}) collective-permute-start(bf16[2,48,512]{2,1,0:T(8,128)(2,1)S(1)} %pad_maximum_fusion.7), channel_id=1, source_target_pairs={{0,6},{2,0},{4,2},{6,4},{1,7},{3,1},{5,3},{7,5},{8,14},{10,8},{12,... | collective-permute-start | bytes 294920 | tf_op jit(solution)/shard_map/ppermute | solution.py:120
  132.9 0.8 collective-permute-start.16
  133.6 2.7 %collective-permute-done.18.three = bf16[2,48,512]{2,1,0:T(8,128)(2,1)S(1)} collective-permute-done((bf16[2,48,512]{2,1,0:T(8,128)(2,1)S(1)}, bf16[2,48,512]{2,1,0:T(8,128)(2,1)S(1)}, u32[]{:S(2)}, u32[]{:S(2)}) %collective-permute-start.18) | collective-permute-done | bytes 98336 | tf_op jit(solution)/shard_map/ppermute | solution.py:120
  136.3 1.8 collective-permute-done.17.two
  138.1 2.3 %collective-permute-done.16.one = bf16[2,48,512]{2,1,0:T(8,128)(2,1)S(1)} collective-permute-done((bf16[2,48,512]{2,1,0:T(8,128)(2,1)S(1)}, bf16[2,48,512]{2,1,0:T(8,128)(2,1)S(1)}, u32[]{:S(2)}, u32[]{:S(2)}) %collective-permute-start.16) | collective-permute-done | bytes 98336 | tf_op jit(solution)/shard_map/ppermute | solution.py:120
  140.4 1.2 collect.3.refs_0_
  141.6 0.9 collective-permute-start.23
  143.4 5.2 %collective-permute-done.23 = bf16[8,48,512]{2,1,0:T(8,128)(2,1)S(1)} collective-permute-done((bf16[8,48,512]{2,1,0:T(8,128)(2,1)S(1)}, bf16[8,48,512]{2,1,0:T(8,128)(2,1)S(1)}, u32[]{:S(2)}, u32[]{:S(2)}) %collective-permute-start.23) | collective-permute-done | bytes 393248 | tf_op jit(solution)/shard_map/ppermute | solution.py:221
  149.1 2.5 %collective-permute-start.30 = (bf16[16,48,512]{2,1,0:T(8,128)(2,1)S(1)}, bf16[16,48,512]{2,1,0:T(8,128)(2,1)S(1)}, u32[]{:S(2)}, u32[]{:S(2)}) collective-permute-start(bf16[16,48,512]{2,1,0:T(8,128)(2,1)S(1)} %collective-permute-done.19.refs_1_.refs_2_), channel_id=1, source_target_pairs={{0,8},{8,0},{1,9},{9,1},{2,10},{10,2},{3,11},{11,3},{4,12},{12,4},... | collective-permute-start | bytes 2359304 | tf_op jit(solution)/shard_map/ppermute | solution.py:236
  151.6 1.7 collective-permute-done.20
  154.0 10.5 %collective-permute-done.21 = bf16[8,48,512]{2,1,0:T(8,128)(2,1)S(1)} collective-permute-done((bf16[8,48,512]{2,1,0:T(8,128)(2,1)S(1)}, bf16[8,48,512]{2,1,0:T(8,128)(2,1)S(1)}, u32[]{:S(2)}, u32[]{:S(2)}) %collective-permute-start.21) | collective-permute-done | bytes 393248 | tf_op jit(solution)/shard_map/ppermute | solution.py:221
  164.5 1.5 collective-permute-start.24
  166.6 1.1 collective-permute-start.27
  168.3 0.8 collective-permute-done.32.refs_7_
  169.0 3.9 %place_0.1 = (bf16[8,16,96,512]{3,2,1,0:T(8,128)(2,1)}, f32[8,128]{1,0:T(8,128)}) custom-call(s32[5]{0:T(128)S(1)} %stack.41.where.refs_0_, bf16[16,48,512]{2,1,0:T(8,128)(2,1)S(1)} %pad_maximum_fusion.refs_1_.refs_0_, bf16[16,48,512]{2,1,0:T(8,128)(2,1)S(1)} %collective-permute-done.29.refs_1_, ...), custom_call_target="tpu_custom_call" | custom-call | tf_op jit(solution)/shard_map/place_0/pallas_call | solution.py:176
  173.0 2.8 %place_1.2 = (bf16[8,16,96,512]{3,2,1,0:T(8,128)(2,1)}, f32[8,128]{1,0:T(8,128)S(1)}) custom-call(s32[5]{0:T(128)S(1)} %stack.41.where.refs_0_, bf16[16,48,512]{2,1,0:T(8,128)(2,1)S(1)} %pad_maximum_fusion.1.refs_0_, bf16[16,48,512]{2,1,0:T(8,128)(2,1)S(1)} %collective-permute-done.24.refs_1_, ...), custom_call_target="tpu_custom_call", output_to_operand_aliasing={{0}: (7, {})} | custom-call | tf_op jit(solution)/shard_map/place_1/pallas_call | solution.py:176
  175.8 3.9 %collective-permute-done.22.refs_0_ = bf16[16,48,512]{2,1,0:T(8,128)(2,1)S(1)} collective-permute-done((bf16[16,48,512]{2,1,0:T(8,128)(2,1)S(1)}, bf16[16,48,512]{2,1,0:T(8,128)(2,1)S(1)}, u32[]{:S(2)}, u32[]{:S(2)}) %collective-permute-start.22) | collective-permute-done | bytes 786464 | tf_op jit(solution)/shard_map/ppermute | solution.py:221
  179.8 2.3 %collective-permute-done.33.refs_1_ = bf16[16,48,512]{2,1,0:T(8,128)(2,1)S(1)} collective-permute-done((bf16[16,48,512]{2,1,0:T(8,128)(2,1)S(1)}, bf16[16,48,512]{2,1,0:T(8,128)(2,1)S(1)}, u32[]{:S(2)}, u32[]{:S(2)}) %collective-permute-start.33) | collective-permute-done | bytes 786464 | tf_op jit(solution)/shard_map/ppermute | solution.py:236
  182.1 2.3 %place_1.3 = (bf16[8,16,96,512]{3,2,1,0:T(8,128)(2,1)}, f32[8,128]{1,0:T(8,128)}) custom-call(s32[5]{0:T(128)S(1)} %stack.41.where.refs_0_, bf16[16,48,512]{2,1,0:T(8,128)(2,1)S(1)} %after.17.refs_0_, bf16[16,48,512]{2,1,0:T(8,128)(2,1)S(1)} %collective-permute-done.33.refs_1_, ...), custom_call_target="tpu_custom_call", output_to_operand_aliasing={{0}: (3, {})} | custom-call | tf_op jit(solution)/shard_map/place_1/pallas_call | solution.py:176
  (82 shorter events, 10.2 us)
Async XLA Ops:
  0.7 2.8 %copy-start = (bf16[2048,1536]{1,0:T(8,128)(2,1)S(1)}, bf16[2048,1536]{1,0:T(8,128)(2,1)}, u32[]{:S(2)}) copy-start(bf16[2048,1536]{1,0:T(8,128)(2,1)} %grads.1) | copy-start | bytes 18874372
  18.4 11.8 %collective-permute-start = (f16[384,4096]{1,0:T(8,128)(2,1)S(1)}, f16[384,4096]{1,0:T(8,128)(2,1)S(1)}, u32[]{:S(2)}, u32[]{:S(2)}) collective-permute-start(f16[384,4096]{1,0:T(8,128)(2,1)S(1)} %convolution_convert_fusion.1), channel_id=1, source_target_pairs={{0,8},{8,0},{1,9},{9,1},{2,10},{10,2},{3,11},{11,3},{4,12},{12,4},... | collective-permute-start | bytes 9437192 | tf_op jit(solution)/shard_map/ppermute | solution.py:269
  30.6 20.6 %collective-permute-start.1 = (f16[192,4096]{1,0:T(8,128)(2,1)S(1)}, f16[192,4096]{1,0:T(8,128)(2,1)S(1)}, u32[]{:S(2)}, u32[]{:S(2)}) collective-permute-start(f16[192,4096]{1,0:T(8,128)(2,1)S(1)} %fusion.1), channel_id=1, source_target_pairs={{0,32},{8,104},{32,0},{40,72},{64,96},{72,40},{96,64},{104,8},{1,3... | collective-permute-start | bytes 4718600 | tf_op jit(solution)/shard_map/ppermute | solution.py:221
  43.5 21.6 %collective-permute-start.2 = (f16[384,4096]{1,0:T(8,128)(2,1)S(1)}, f16[384,4096]{1,0:T(8,128)(2,1)S(1)}, u32[]{:S(2)}, u32[]{:S(2)}) collective-permute-start(f16[384,4096]{1,0:T(8,128)(2,1)S(1)} %convolution_convert_fusion), channel_id=1, source_target_pairs={{0,8},{8,0},{1,9},{9,1},{2,10},{10,2},{3,11},{11,3},{4,12},{12,4},... | collective-permute-start | bytes 9437192 | tf_op jit(solution)/shard_map/ppermute | solution.py:272
  51.4 11.4 %collective-permute-start.4 = (f16[96,4096]{1,0:T(8,128)(2,1)S(1)}, f16[96,4096]{1,0:T(8,128)(2,1)S(1)}, u32[]{:S(2)}, u32[]{:S(2)}) collective-permute-start(f16[96,4096]{1,0:T(8,128)(2,1)S(1)} %fusion.10), channel_id=1, source_target_pairs={{0,96},{8,40},{32,64},{40,8},{64,32},{72,104},{96,0},{104,72},{1,9... | collective-permute-start | bytes 2359304 | tf_op jit(solution)/shard_map/ppermute | solution.py:221
  63.3 9.2 %collective-permute-start.5 = (f16[48,4096]{1,0:T(8,128)(2,1)S(1)}, f16[48,4096]{1,0:T(8,128)(2,1)S(1)}, u32[]{:S(2)}, u32[]{:S(2)}) collective-permute-start(f16[48,4096]{1,0:T(8,128)(2,1)S(1)} %slice_convert_fusion.1), channel_id=1, source_target_pairs={{0,16},{16,0},{1,17},{17,1},{2,18},{18,2},{3,19},{19,3},{4,20},{20... | collective-permute-start | bytes 1179656 | tf_op jit(solution)/shard_map/ppermute | solution.py:263
  65.1 7.5 %copy-start.3 = (f32[1,96,4096]{2,1,0:T(8,128)S(1)}, f32[1,96,4096]{2,1,0:T(8,128)}, u32[]{:S(2)}) copy-start(f32[1,96,4096]{2,1,0:T(8,128)} %param.9) | copy-start | bytes 4718596
  65.5 20.6 %collective-permute-start.3 = (f16[192,4096]{1,0:T(8,128)(2,1)S(1)}, f16[192,4096]{1,0:T(8,128)(2,1)S(1)}, u32[]{:S(2)}, u32[]{:S(2)}) collective-permute-start(f16[192,4096]{1,0:T(8,128)(2,1)S(1)} %fusion), channel_id=1, source_target_pairs={{0,32},{8,104},{32,0},{40,72},{64,96},{72,40},{96,64},{104,8},{1,3... | collective-permute-start | bytes 4718600 | tf_op jit(solution)/shard_map/ppermute | solution.py:221
  68.1 4.5 %copy-start.1 = (f32[1,96,4096]{2,1,0:T(8,128)S(1)}, f32[1,96,4096]{2,1,0:T(8,128)}, u32[]{:S(2)}) copy-start(f32[1,96,4096]{2,1,0:T(8,128)} %param.7) | copy-start | bytes 4718596
  68.1 4.5 %copy-start.2 = (f32[1,96,4096]{2,1,0:T(8,128)S(1)}, f32[1,96,4096]{2,1,0:T(8,128)}, u32[]{:S(2)}) copy-start(f32[1,96,4096]{2,1,0:T(8,128)} %param.8) | copy-start | bytes 4718596
  76.0 10.7 %collective-permute-start.8 = (bf16[4,48,512]{2,1,0:T(8,128)(2,1)S(1)}, bf16[4,48,512]{2,1,0:T(8,128)(2,1)S(1)}, u32[]{:S(2)}, u32[]{:S(2)}) collective-permute-start(bf16[4,48,512]{2,1,0:T(8,128)(2,1)S(1)} %slice_bitcast_fusion.1), channel_id=1, source_target_pairs={{0,1},{1,0},{2,3},{3,2},{4,5},{5,4},{6,7},{7,6},{8,9},{9,8},{10,11... | collective-permute-start | bytes 589832 | tf_op jit(solution)/shard_map/ppermute | solution.py:118
  86.4 11.2 %collective-permute-start.6 = (f16[96,4096]{1,0:T(8,128)(2,1)S(1)}, f16[96,4096]{1,0:T(8,128)(2,1)S(1)}, u32[]{:S(2)}, u32[]{:S(2)}) collective-permute-start(f16[96,4096]{1,0:T(8,128)(2,1)S(1)} %fusion.6), channel_id=1, source_target_pairs={{0,96},{8,40},{32,64},{40,8},{64,32},{72,104},{96,0},{104,72},{1,9... | collective-permute-start | bytes 2359304 | tf_op jit(solution)/shard_map/ppermute | solution.py:221
  86.7 4.4 %collective-permute-start.11 = (bf16[2,48,512]{2,1,0:T(8,128)(2,1)S(1)}, bf16[2,48,512]{2,1,0:T(8,128)(2,1)S(1)}, u32[]{:S(2)}, u32[]{:S(2)}) collective-permute-start(bf16[2,48,512]{2,1,0:T(8,128)(2,1)S(1)} %pad_maximum_fusion.4), channel_id=1, source_target_pairs={{0,6},{2,0},{4,2},{6,4},{1,7},{3,1},{5,3},{7,5},{8,14},{10,8},{12,... | collective-permute-start | bytes 294920 | tf_op jit(solution)/shard_map/ppermute | solution.py:120
  89.5 5.1 %collective-permute-start.10 = (bf16[2,48,512]{2,1,0:T(8,128)(2,1)S(1)}, bf16[2,48,512]{2,1,0:T(8,128)(2,1)S(1)}, u32[]{:S(2)}, u32[]{:S(2)}) collective-permute-start(bf16[2,48,512]{2,1,0:T(8,128)(2,1)S(1)} %pad_maximum_fusion.3), channel_id=1, source_target_pairs={{0,4},{2,6},{4,0},{6,2},{1,5},{3,7},{5,1},{7,3},{8,12},{10,14},{12... | collective-permute-start | bytes 294920 | tf_op jit(solution)/shard_map/ppermute | solution.py:120
  90.0 6.0 %collective-permute-start.9 = (bf16[2,48,512]{2,1,0:T(8,128)(2,1)S(1)}, bf16[2,48,512]{2,1,0:T(8,128)(2,1)S(1)}, u32[]{:S(2)}, u32[]{:S(2)}) collective-permute-start(bf16[2,48,512]{2,1,0:T(8,128)(2,1)S(1)} %pad_maximum_fusion.2), channel_id=1, source_target_pairs={{0,2},{2,4},{4,6},{6,0},{1,3},{3,5},{5,7},{7,1},{8,10},{10,12},{12... | collective-permute-start | bytes 294920 | tf_op jit(solution)/shard_map/ppermute | solution.py:120
  98.1 6.7 %collective-permute-start.12 = (bf16[8,48,512]{2,1,0:T(8,128)(2,1)S(1)}, bf16[8,48,512]{2,1,0:T(8,128)(2,1)S(1)}, u32[]{:S(2)}, u32[]{:S(2)}) collective-permute-start(bf16[8,48,512]{2,1,0:T(8,128)(2,1)S(1)} %after.12), channel_id=1, source_target_pairs={{0,96},{8,40},{32,64},{40,8},{64,32},{72,104},{96,0},{104,72},{1,9... | collective-permute-start | bytes 1179656 | tf_op jit(solution)/shard_map/ppermute | solution.py:221
  98.7 9.5 %collective-permute-start.7 = (f16[48,4096]{1,0:T(8,128)(2,1)S(1)}, f16[48,4096]{1,0:T(8,128)(2,1)S(1)}, u32[]{:S(2)}, u32[]{:S(2)}) collective-permute-start(f16[48,4096]{1,0:T(8,128)(2,1)S(1)} %slice_convert_fusion), channel_id=1, source_target_pairs={{0,16},{16,0},{1,17},{17,1},{2,18},{18,2},{3,19},{19,3},{4,20},{20... | collective-permute-start | bytes 1179656 | tf_op jit(solution)/shard_map/ppermute | solution.py:263
  98.9 12.3 %collective-permute-start.14 = (bf16[8,48,512]{2,1,0:T(8,128)(2,1)S(1)}, bf16[8,48,512]{2,1,0:T(8,128)(2,1)S(1)}, u32[]{:S(2)}, u32[]{:S(2)}) collective-permute-start(bf16[8,48,512]{2,1,0:T(8,128)(2,1)S(1)} %after.12), channel_id=1, source_target_pairs={{0,16},{16,0},{1,17},{17,1},{2,18},{18,2},{3,19},{19,3},{4,20},{20... | collective-permute-start | bytes 1179656 | tf_op jit(solution)/shard_map/ppermute | solution.py:225
  104.8 36.7 %collective-permute-start.19 = (bf16[16,48,512]{2,1,0:T(8,128)(2,1)S(1)}, bf16[16,48,512]{2,1,0:T(8,128)(2,1)S(1)}, u32[]{:S(2)}, u32[]{:S(2)}) collective-permute-start(bf16[16,48,512]{2,1,0:T(8,128)(2,1)S(1)} %pad_maximum_fusion.refs_1_.refs_0_), channel_id=1, source_target_pairs={{0,32},{8,104},{32,0},{40,72},{64,96},{72,40},{96,64},{104,8},{1,3... | collective-permute-start | bytes 2359304 | tf_op jit(solution)/shard_map/ppermute | solution.py:221
  111.2 11.7 %collective-permute-start.15 = (bf16[8,48,512]{2,1,0:T(8,128)(2,1)S(1)}, bf16[8,48,512]{2,1,0:T(8,128)(2,1)S(1)}, u32[]{:S(2)}, u32[]{:S(2)}) collective-permute-start(bf16[8,48,512]{2,1,0:T(8,128)(2,1)S(1)} %collective-permute-done.14), channel_id=1, source_target_pairs={{0,96},{8,40},{32,64},{40,8},{64,32},{72,104},{96,0},{104,72},{1,9... | collective-permute-start | bytes 1179656 | tf_op jit(solution)/shard_map/ppermute | solution.py:221
  114.8 14.9 %collective-permute-start.13 = (bf16[4,48,512]{2,1,0:T(8,128)(2,1)S(1)}, bf16[4,48,512]{2,1,0:T(8,128)(2,1)S(1)}, u32[]{:S(2)}, u32[]{:S(2)}) collective-permute-start(bf16[4,48,512]{2,1,0:T(8,128)(2,1)S(1)} %slice_bitcast_fusion), channel_id=1, source_target_pairs={{0,1},{1,0},{2,3},{3,2},{4,5},{5,4},{6,7},{7,6},{8,9},{9,8},{10,11... | collective-permute-start | bytes 589832 | tf_op jit(solution)/shard_map/ppermute | solution.py:118
  122.9 25.8 %collective-permute-start.25 = (bf16[16,48,512]{2,1,0:T(8,128)(2,1)S(1)}, bf16[16,48,512]{2,1,0:T(8,128)(2,1)S(1)}, u32[]{:S(2)}, u32[]{:S(2)}) collective-permute-start(bf16[16,48,512]{2,1,0:T(8,128)(2,1)S(1)} %constant_dynamic-update-slice_fusion.refs_1_.refs_4_), channel_id=1, source_target_pairs={{0,32},{8,104},{32,0},{40,72},{64,96},{72,40},{96,64},{104,8},{1,3... | collective-permute-start | bytes 2359304 | tf_op jit(solution)/shard_map/ppermute | solution.py:221
  129.7 6.6 %collective-permute-start.18 = (bf16[2,48,512]{2,1,0:T(8,128)(2,1)S(1)}, bf16[2,48,512]{2,1,0:T(8,128)(2,1)S(1)}, u32[]{:S(2)}, u32[]{:S(2)}) collective-permute-start(bf16[2,48,512]{2,1,0:T(8,128)(2,1)S(1)} %pad_maximum_fusion.7), channel_id=1, source_target_pairs={{0,6},{2,0},{4,2},{6,4},{1,7},{3,1},{5,3},{7,5},{8,14},{10,8},{12,... | collective-permute-start | bytes 294920 | tf_op jit(solution)/shard_map/ppermute | solution.py:120
  132.4 5.7 %collective-permute-start.17 = (bf16[2,48,512]{2,1,0:T(8,128)(2,1)S(1)}, bf16[2,48,512]{2,1,0:T(8,128)(2,1)S(1)}, u32[]{:S(2)}, u32[]{:S(2)}) collective-permute-start(bf16[2,48,512]{2,1,0:T(8,128)(2,1)S(1)} %pad_maximum_fusion.6), channel_id=1, source_target_pairs={{0,4},{2,6},{4,0},{6,2},{1,5},{3,7},{5,1},{7,3},{8,12},{10,14},{12... | collective-permute-start | bytes 294920 | tf_op jit(solution)/shard_map/ppermute | solution.py:120
  132.9 7.5 %collective-permute-start.16 = (bf16[2,48,512]{2,1,0:T(8,128)(2,1)S(1)}, bf16[2,48,512]{2,1,0:T(8,128)(2,1)S(1)}, u32[]{:S(2)}, u32[]{:S(2)}) collective-permute-start(bf16[2,48,512]{2,1,0:T(8,128)(2,1)S(1)} %pad_maximum_fusion.5), channel_id=1, source_target_pairs={{0,2},{2,4},{4,6},{6,0},{1,3},{3,5},{5,7},{7,1},{8,10},{10,12},{12... | collective-permute-start | bytes 294920 | tf_op jit(solution)/shard_map/ppermute | solution.py:120
  141.6 7.0 %collective-permute-start.23 = (bf16[8,48,512]{2,1,0:T(8,128)(2,1)S(1)}, bf16[8,48,512]{2,1,0:T(8,128)(2,1)S(1)}, u32[]{:S(2)}, u32[]{:S(2)}) collective-permute-start(bf16[8,48,512]{2,1,0:T(8,128)(2,1)S(1)} %after.15), channel_id=1, source_target_pairs={{0,96},{8,40},{32,64},{40,8},{64,32},{72,104},{96,0},{104,72},{1,9... | collective-permute-start | bytes 1179656 | tf_op jit(solution)/shard_map/ppermute | solution.py:221
  142.5 23.5 %collective-permute-start.29 = (bf16[16,48,512]{2,1,0:T(8,128)(2,1)S(1)}, bf16[16,48,512]{2,1,0:T(8,128)(2,1)S(1)}, u32[]{:S(2)}, u32[]{:S(2)}) collective-permute-start(bf16[16,48,512]{2,1,0:T(8,128)(2,1)S(1)} %pad_maximum_fusion.refs_1_.refs_0_), channel_id=1, source_target_pairs={{0,8},{8,0},{1,9},{9,1},{2,10},{10,2},{3,11},{11,3},{4,12},{12,4},... | collective-permute-start | bytes 2359304 | tf_op jit(solution)/shard_map/ppermute | solution.py:236
  142.9 23.2 %collective-permute-start.31 = (bf16[16,48,512]{2,1,0:T(8,128)(2,1)S(1)}, bf16[16,48,512]{2,1,0:T(8,128)(2,1)S(1)}, u32[]{:S(2)}, u32[]{:S(2)}) collective-permute-start(bf16[16,48,512]{2,1,0:T(8,128)(2,1)S(1)} %constant_dynamic-update-slice_fusion.refs_1_.refs_4_), channel_id=1, source_target_pairs={{0,8},{8,0},{1,9},{9,1},{2,10},{10,2},{3,11},{11,3},{4,12},{12,4},... | collective-permute-start | bytes 2359304 | tf_op jit(solution)/shard_map/ppermute | solution.py:236
  143.0 10.3 %collective-permute-start.20 = (bf16[8,48,512]{2,1,0:T(8,128)(2,1)S(1)}, bf16[8,48,512]{2,1,0:T(8,128)(2,1)S(1)}, u32[]{:S(2)}, u32[]{:S(2)}) collective-permute-start(bf16[8,48,512]{2,1,0:T(8,128)(2,1)S(1)} %after.15), channel_id=1, source_target_pairs={{0,16},{16,0},{1,17},{17,1},{2,18},{18,2},{3,19},{19,3},{4,20},{20... | collective-permute-start | bytes 1179656 | tf_op jit(solution)/shard_map/ppermute | solution.py:225
  148.7 17.9 %collective-permute-start.26 = (bf16[16,48,512]{2,1,0:T(8,128)(2,1)S(1)}, bf16[16,48,512]{2,1,0:T(8,128)(2,1)S(1)}, u32[]{:S(2)}, u32[]{:S(2)}) collective-permute-start(bf16[16,48,512]{2,1,0:T(8,128)(2,1)S(1)} %after.16), channel_id=1, source_target_pairs={{0,32},{8,104},{32,0},{40,72},{64,96},{72,40},{96,64},{104,8},{1,3... | collective-permute-start | bytes 2359304 | tf_op jit(solution)/shard_map/ppermute | solution.py:221
  149.1 18.6 %collective-permute-start.30 = (bf16[16,48,512]{2,1,0:T(8,128)(2,1)S(1)}, bf16[16,48,512]{2,1,0:T(8,128)(2,1)S(1)}, u32[]{:S(2)}, u32[]{:S(2)}) collective-permute-start(bf16[16,48,512]{2,1,0:T(8,128)(2,1)S(1)} %collective-permute-done.19.refs_1_.refs_2_), channel_id=1, source_target_pairs={{0,8},{8,0},{1,9},{9,1},{2,10},{10,2},{3,11},{11,3},{4,12},{12,4},... | collective-permute-start | bytes 2359304 | tf_op jit(solution)/shard_map/ppermute | solution.py:236
  153.3 11.2 %collective-permute-start.21 = (bf16[8,48,512]{2,1,0:T(8,128)(2,1)S(1)}, bf16[8,48,512]{2,1,0:T(8,128)(2,1)S(1)}, u32[]{:S(2)}, u32[]{:S(2)}) collective-permute-start(bf16[8,48,512]{2,1,0:T(8,128)(2,1)S(1)} %collective-permute-done.20), channel_id=1, source_target_pairs={{0,96},{8,40},{32,64},{40,8},{64,32},{72,104},{96,0},{104,72},{1,9... | collective-permute-start | bytes 1179656 | tf_op jit(solution)/shard_map/ppermute | solution.py:221
  164.5 8.5 %collective-permute-start.24 = (bf16[16,48,512]{2,1,0:T(8,128)(2,1)S(1)}, bf16[16,48,512]{2,1,0:T(8,128)(2,1)S(1)}, u32[]{:S(2)}, u32[]{:S(2)}) collective-permute-start(bf16[16,48,512]{2,1,0:T(8,128)(2,1)S(1)} %pad_maximum_fusion.1.refs_0_), channel_id=1, source_target_pairs={{0,8},{8,0},{1,9},{9,1},{2,10},{10,2},{3,11},{11,3},{4,12},{12,4},... | collective-permute-start | bytes 2359304 | tf_op jit(solution)/shard_map/ppermute | solution.py:236
  166.0 3.0 %collective-permute-start.32 = (bf16[16,48,512]{2,1,0:T(8,128)(2,1)S(1)}, bf16[16,48,512]{2,1,0:T(8,128)(2,1)S(1)}, u32[]{:S(2)}, u32[]{:S(2)}) collective-permute-start(bf16[16,48,512]{2,1,0:T(8,128)(2,1)S(1)} %collective-permute-done.25.refs_1_.refs_6_), channel_id=1, source_target_pairs={{0,8},{8,0},{1,9},{9,1},{2,10},{10,2},{3,11},{11,3},{4,12},{12,4},... | collective-permute-start | bytes 2359304 | tf_op jit(solution)/shard_map/ppermute | solution.py:236
  166.1 6.8 %collective-permute-start.28 = (bf16[16,48,512]{2,1,0:T(8,128)(2,1)S(1)}, bf16[16,48,512]{2,1,0:T(8,128)(2,1)S(1)}, u32[]{:S(2)}, u32[]{:S(2)}) collective-permute-start(bf16[16,48,512]{2,1,0:T(8,128)(2,1)S(1)} %constant_dynamic-update-slice_fusion.2.refs_8_.refs_4_), channel_id=1, source_target_pairs={{0,8},{8,0},{1,9},{9,1},{2,10},{10,2},{3,11},{11,3},{4,12},{12,4},... | collective-permute-start | bytes 2359304 | tf_op jit(solution)/shard_map/ppermute | solution.py:236
  166.6 6.4 %collective-permute-start.27 = (bf16[16,48,512]{2,1,0:T(8,128)(2,1)S(1)}, bf16[16,48,512]{2,1,0:T(8,128)(2,1)S(1)}, u32[]{:S(2)}, u32[]{:S(2)}) collective-permute-start(bf16[16,48,512]{2,1,0:T(8,128)(2,1)S(1)} %collective-permute-done.26.refs_2_), channel_id=1, source_target_pairs={{0,8},{8,0},{1,9},{9,1},{2,10},{10,2},{3,11},{11,3},{4,12},{12,4},... | collective-permute-start | bytes 2359304 | tf_op jit(solution)/shard_map/ppermute | solution.py:236
  167.7 12.1 %collective-permute-start.22 = (bf16[16,48,512]{2,1,0:T(8,128)(2,1)S(1)}, bf16[16,48,512]{2,1,0:T(8,128)(2,1)S(1)}, u32[]{:S(2)}, u32[]{:S(2)}) collective-permute-start(bf16[16,48,512]{2,1,0:T(8,128)(2,1)S(1)} %constant_dynamic-update-slice_fusion.2.refs_8_.refs_4_), channel_id=1, source_target_pairs={{0,32},{8,104},{32,0},{40,72},{64,96},{72,40},{96,64},{104,8},{1,3... | collective-permute-start | bytes 2359304 | tf_op jit(solution)/shard_map/ppermute | solution.py:221
  179.8 2.3 %collective-permute-start.33 = (bf16[16,48,512]{2,1,0:T(8,128)(2,1)S(1)}, bf16[16,48,512]{2,1,0:T(8,128)(2,1)S(1)}, u32[]{:S(2)}, u32[]{:S(2)}) collective-permute-start(bf16[16,48,512]{2,1,0:T(8,128)(2,1)S(1)} %after.17.refs_0_), channel_id=1, source_target_pairs={{0,8},{8,0},{1,9},{9,1},{2,10},{10,2},{3,11},{11,3},{4,12},{12,4},... | collective-permute-start | bytes 2359304 | tf_op jit(solution)/shard_map/ppermute | solution.py:236

commit v2 on v1

--- a/solution.py
+++ b/solution.py
@@ -71,7 +71,7 @@
             ],
         ),
         out_shape=[jax.ShapeDtypeStruct((4, 2, count, 2048), BF16) for count in CHUNKS for _ in range(2)],
-        compiler_params=params(14),
+        compiler_params=params(48),
         name="order_rows",
     )(where, logit_grads)
 

time: 185 us -> 184 us (level)
  local copies, waits for them, and re-layouts: 3.62 us -> 0.84 us
  Pallas kernels: 21.7 us -> 24 us
    unnamed x11, local copies, waits for them, and re-layouts: 2.9 us -> 0.12 us
    pallas_call x1, Pallas kernels: 4.54 us -> 6.81 us  [order_rows(): pl.pallas_call(order_kernel, grid_spec=pltpu.PrefetchScalarGridSpec(num_s...]
where the time goes in v2:
time: 184 us
  waiting for transfers between devices  64.8 us (35%)
  starting transfers between devices  48.7 us (26%)
  matrix products  41.1 us (22%)
  Pallas kernels  24 us (13%)
  other arithmetic  2.78 us (2%)
  between operations  1.87 us (1%)
    ppermute x12, waiting for transfers between devices, swap(): return lax.ppermute(a, ('x', 'c'), SWAPS[k])  43.6 us
    dot_general x4, matrix products, dot(): return jnp.dot(a, b, preferred_element_type=F32)  41.1 us
    ppermute x12, starting transfers between devices, swap(): return lax.ppermute(a, ('x', 'c'), SWAPS[k])  22.8 us
    ppermute x6, waiting for transfers between devices, exchange(): lax.ppermute(jnp.stack([rounded[0, k], got[k]]), 'y', [(i, (i + k) % 4) f...  12 us
    pallas_call x3, Pallas kernels, place(): pl.pallas_call(kernel, grid_spec=pltpu.PrefetchScalarGridSpec(num_scalar_...  9.06 us
    ppermute x6, starting transfers between devices, exchange(): lax.ppermute(jnp.stack([rounded[0, k], got[k]]), 'y', [(i, (i + k) % 4) f...  7.86 us
    pallas_call x1, Pallas kernels, order_rows(): pl.pallas_call(order_kernel, grid_spec=pltpu.PrefetchScalarGridSpec(num_s...  6.81 us
    ppermute x2, starting transfers between devices, exchange(): got = after(lax.ppermute(rounded[1], 'zh', SWAP), *gate)  6.63 us
  transfers between devices with their start and end apart: 34, of which 19 were waited for; matrix products, arithmetic and copies ran while one was open for 18% of the time, Pallas kernels for 8%

profile of v2, /device:TPU:1, one launch (start us, length us, event | category | flops | bytes accessed | tf_op | source)
XLA Modules:
  0.0 184.0 jit_solution(17236478468387889486)
XLA Ops:
  0.7 6.8 %order_rows.1 = (bf16[4,2,48,2048]{3,2,1,0:T(8,128)(2,1)S(1)}, bf16[4,2,48,2048]{3,2,1,0:T(8,128)(2,1)S(1)}, bf16[4,2,48,2048]{3,2,1,0:T(8,128)(2,1)S(1)}, bf16[4,2,48,2048]{3,2,1,0:T(8,128)(2,1)}) custom-call(s32[5]{0:T(128)S(1)} %stack.41.where.refs_0_, bf16[2048,1536]{1,0:T(8,128)(2,1)} %grads.1), custom_call_target="tpu_custom_call" | custom-call | tf_op jit(solution)/shard_map/order_rows/pallas_call | solution.py:58
  7.5 10.3 %convolution_convert_fusion.1 = f16[384,4096]{1,0:T(8,128)(2,1)S(1)} fusion(bf16[384,2048]{1,0:T(8,128)(2,1)S(1)} %bitcast.50, bf16[2048,4096]{1,0:T(8,128)(2,1)} %param.5), kind=kOutput, calls=%fused_computation.1 | convolution fusion | flops 6444023808 | bytes 21495808 | tf_op jit(solution)/shard_map/dot_general | solution.py:217
  17.9 1.5 collective-permute-start
  19.3 10.3 %fusion.13.refs_1_ = f32[384,4096]{1,0:T(8,128)S(1)} fusion(bf16[384,2048]{1,0:T(8,128)(2,1)S(1)} %bitcast.49, bf16[2048,4096]{1,0:T(8,128)(2,1)} %param.5), kind=kOutput, calls=%fused_computation.47 | convolution fusion | flops 6442450944 | bytes 24641536 | tf_op jit(solution)/shard_map/dot_general | solution.py:217
  30.1 2.6 %collective-permute-start.1 = (f16[192,4096]{1,0:T(8,128)(2,1)S(1)}, f16[192,4096]{1,0:T(8,128)(2,1)S(1)}, u32[]{:S(2)}, u32[]{:S(2)}) collective-permute-start(f16[192,4096]{1,0:T(8,128)(2,1)S(1)} %fusion.1), channel_id=1, source_target_pairs={{0,32},{8,104},{32,0},{40,72},{64,96},{72,40},{96,64},{104,8},{1,3... | collective-permute-start | bytes 4718600 | tf_op jit(solution)/shard_map/ppermute | solution.py:221
  32.7 10.3 %convolution_convert_fusion = f16[384,4096]{1,0:T(8,128)(2,1)S(1)} fusion(bf16[384,2048]{1,0:T(8,128)(2,1)S(1)} %after.10, bf16[2048,4096]{1,0:T(8,128)(2,1)} %param.5), kind=kOutput, calls=%fused_computation | convolution fusion | flops 6444023808 | bytes 21495808 | tf_op jit(solution)/shard_map/dot_general | solution.py:217
  43.1 7.5 %collective-permute-done.1 = f16[192,4096]{1,0:T(8,128)(2,1)S(1)} collective-permute-done((f16[192,4096]{1,0:T(8,128)(2,1)S(1)}, f16[192,4096]{1,0:T(8,128)(2,1)S(1)}, u32[]{:S(2)}, u32[]{:S(2)}) %collective-permute-start.1) | collective-permute-done | bytes 1572896 | tf_op jit(solution)/shard_map/ppermute | solution.py:221
  50.9 0.6 collective-permute-start.4
  51.6 10.3 %fusion.14 = f32[384,4096]{1,0:T(8,128)S(1)} fusion(bf16[384,2048]{1,0:T(8,128)(2,1)S(1)} %after.9, bf16[2048,4096]{1,0:T(8,128)(2,1)} %param.5), kind=kOutput, calls=%fused_computation.48 | convolution fusion | flops 6442450944 | bytes 24641536 | tf_op jit(solution)/shard_map/dot_general | solution.py:217
  62.8 1.8 collective-permute-start.5
  65.0 2.6 %collective-permute-start.3 = (f16[192,4096]{1,0:T(8,128)(2,1)S(1)}, f16[192,4096]{1,0:T(8,128)(2,1)S(1)}, u32[]{:S(2)}, u32[]{:S(2)}) collective-permute-start(f16[192,4096]{1,0:T(8,128)(2,1)S(1)} %fusion), channel_id=1, source_target_pairs={{0,32},{8,104},{32,0},{40,72},{64,96},{72,40},{96,64},{104,8},{1,3... | collective-permute-start | bytes 4718600 | tf_op jit(solution)/shard_map/ppermute | solution.py:221
  67.6 4.4 %collective-permute-done.5 = f16[48,4096]{1,0:T(8,128)(2,1)S(1)} collective-permute-done((f16[48,4096]{1,0:T(8,128)(2,1)S(1)}, f16[48,4096]{1,0:T(8,128)(2,1)S(1)}, u32[]{:S(2)}, u32[]{:S(2)}) %collective-permute-start.5) | collective-permute-done | bytes 393248 | tf_op jit(solution)/shard_map/ppermute | solution.py:263
  72.1 2.9 %adam_0.1 = (f32[96,4096]{1,0:T(8,128)}, f32[96,4096]{1,0:T(8,128)}, f32[96,4096]{1,0:T(8,128)}, bf16[2,4,48,512]{3,2,1,0:T(8,128)(2,1)S(1)}) custom-call(s32[5]{0:T(128)S(1)} %stack.41.where.refs_0_, f32[48,4096]{1,0:T(8,128)S(1)} %after.11.refs_1_, f32[96,4096]{1,0:T(8,128)S(1)} %bitcast.41, f32[96,4096]{1,0:T(8,128)S(1)} %bitcast.43, f32[96,4096]{1,0:T(8,128)S(1)} %bitcast.45), custom_call_target="tpu_custom_call" | custom-call | tf_op jit(solution)/shard_map/adam_0/pallas_call | solution.py:99
  75.5 3.2 %collective-permute-start.8 = (bf16[4,48,512]{2,1,0:T(8,128)(2,1)S(1)}, bf16[4,48,512]{2,1,0:T(8,128)(2,1)S(1)}, u32[]{:S(2)}, u32[]{:S(2)}) collective-permute-start(bf16[4,48,512]{2,1,0:T(8,128)(2,1)S(1)} %slice_bitcast_fusion.1), channel_id=1, source_target_pairs={{0,1},{1,0},{2,3},{3,2},{4,5},{5,4},{6,7},{7,6},{8,9},{9,8},{10,11... | collective-permute-start | bytes 589832 | tf_op jit(solution)/shard_map/ppermute | solution.py:118
  79.4 6.2 %collective-permute-done.3 = f16[192,4096]{1,0:T(8,128)(2,1)S(1)} collective-permute-done((f16[192,4096]{1,0:T(8,128)(2,1)S(1)}, f16[192,4096]{1,0:T(8,128)(2,1)S(1)}, u32[]{:S(2)}, u32[]{:S(2)}) %collective-permute-start.3) | collective-permute-done | bytes 1572896 | tf_op jit(solution)/shard_map/ppermute | solution.py:221
  86.2 2.8 %collective-permute-start.11 = (bf16[2,48,512]{2,1,0:T(8,128)(2,1)S(1)}, bf16[2,48,512]{2,1,0:T(8,128)(2,1)S(1)}, u32[]{:S(2)}, u32[]{:S(2)}) collective-permute-start(bf16[2,48,512]{2,1,0:T(8,128)(2,1)S(1)} %pad_maximum_fusion.4), channel_id=1, source_target_pairs={{0,6},{2,0},{4,2},{6,4},{1,7},{3,1},{5,3},{7,5},{8,14},{10,8},{12,... | collective-permute-start | bytes 294920 | tf_op jit(solution)/shard_map/ppermute | solution.py:120
  89.5 0.8 collective-permute-start.9
  90.6 3.5 %collective-permute-done.10.two = bf16[2,48,512]{2,1,0:T(8,128)(2,1)S(1)} collective-permute-done((bf16[2,48,512]{2,1,0:T(8,128)(2,1)S(1)}, bf16[2,48,512]{2,1,0:T(8,128)(2,1)S(1)}, u32[]{:S(2)}, u32[]{:S(2)}) %collective-permute-start.10) | collective-permute-done | bytes 98336 | tf_op jit(solution)/shard_map/ppermute | solution.py:120
  94.2 1.2 collective-permute-done.9.one
  95.4 1.2 collect.2.refs_0_
  98.4 1.3 collective-permute-start.14
  99.7 4.5 %collective-permute-done.12 = bf16[8,48,512]{2,1,0:T(8,128)(2,1)S(1)} collective-permute-done((bf16[8,48,512]{2,1,0:T(8,128)(2,1)S(1)}, bf16[8,48,512]{2,1,0:T(8,128)(2,1)S(1)}, u32[]{:S(2)}, u32[]{:S(2)}) %collective-permute-start.12) | collective-permute-done | bytes 393248 | tf_op jit(solution)/shard_map/ppermute | solution.py:221
  104.3 3.4 %collective-permute-start.19 = (bf16[16,48,512]{2,1,0:T(8,128)(2,1)S(1)}, bf16[16,48,512]{2,1,0:T(8,128)(2,1)S(1)}, u32[]{:S(2)}, u32[]{:S(2)}) collective-permute-start(bf16[16,48,512]{2,1,0:T(8,128)(2,1)S(1)} %pad_maximum_fusion.refs_1_.refs_0_), channel_id=1, source_target_pairs={{0,32},{8,104},{32,0},{40,72},{64,96},{72,40},{96,64},{104,8},{1,3... | collective-permute-start | bytes 2359304 | tf_op jit(solution)/shard_map/ppermute | solution.py:221
  107.8 2.9 %adam_1.1 = (f32[96,4096]{1,0:T(8,128)}, f32[96,4096]{1,0:T(8,128)}, f32[96,4096]{1,0:T(8,128)}, bf16[2,4,48,512]{3,2,1,0:T(8,128)(2,1)S(1)}) custom-call(s32[5]{0:T(128)S(1)} %stack.41.where.refs_0_, f32[48,4096]{1,0:T(8,128)S(1)} %after.13.refs_1_, f32[96,4096]{1,0:T(8,128)S(1)} %bitcast.42, ...), custom_call_target="tpu_custom_call", output_to_operand_aliasing={{0}: (5, {}), {1}: (6, {}), {2}: (7, {})} | custom-call | tf_op jit(solution)/shard_map/adam_1/pallas_call | solution.py:99
  110.7 3.6 %collective-permute-start.15 = (bf16[8,48,512]{2,1,0:T(8,128)(2,1)S(1)}, bf16[8,48,512]{2,1,0:T(8,128)(2,1)S(1)}, u32[]{:S(2)}, u32[]{:S(2)}) collective-permute-start(bf16[8,48,512]{2,1,0:T(8,128)(2,1)S(1)} %collective-permute-done.14), channel_id=1, source_target_pairs={{0,96},{8,40},{32,64},{40,8},{64,32},{72,104},{96,0},{104,72},{1,9... | collective-permute-start | bytes 1179656 | tf_op jit(solution)/shard_map/ppermute | solution.py:221
  114.3 3.4 %collective-permute-start.13 = (bf16[4,48,512]{2,1,0:T(8,128)(2,1)S(1)}, bf16[4,48,512]{2,1,0:T(8,128)(2,1)S(1)}, u32[]{:S(2)}, u32[]{:S(2)}) collective-permute-start(bf16[4,48,512]{2,1,0:T(8,128)(2,1)S(1)} %slice_bitcast_fusion), channel_id=1, source_target_pairs={{0,1},{1,0},{2,3},{3,2},{4,5},{5,4},{6,7},{7,6},{8,9},{9,8},{10,11... | collective-permute-start | bytes 589832 | tf_op jit(solution)/shard_map/ppermute | solution.py:118
  117.7 4.7 %collective-permute-done.15 = bf16[8,48,512]{2,1,0:T(8,128)(2,1)S(1)} collective-permute-done((bf16[8,48,512]{2,1,0:T(8,128)(2,1)S(1)}, bf16[8,48,512]{2,1,0:T(8,128)(2,1)S(1)}, u32[]{:S(2)}, u32[]{:S(2)}) %collective-permute-start.15) | collective-permute-done | bytes 393248 | tf_op jit(solution)/shard_map/ppermute | solution.py:221
  122.4 6.8 %collective-permute-start.25 = (bf16[16,48,512]{2,1,0:T(8,128)(2,1)S(1)}, bf16[16,48,512]{2,1,0:T(8,128)(2,1)S(1)}, u32[]{:S(2)}, u32[]{:S(2)}) collective-permute-start(bf16[16,48,512]{2,1,0:T(8,128)(2,1)S(1)} %constant_dynamic-update-slice_fusion.refs_1_.refs_4_), channel_id=1, source_target_pairs={{0,32},{8,104},{32,0},{40,72},{64,96},{72,40},{96,64},{104,8},{1,3... | collective-permute-start | bytes 2359304 | tf_op jit(solution)/shard_map/ppermute | solution.py:221
  129.2 2.7 %collective-permute-start.18 = (bf16[2,48,512]{2,1,0:T(8,128)(2,1)S(1)}, bf16[2,48,512]{2,1,0:T(8,128)(2,1)S(1)}, u32[]{:S(2)}, u32[]{:S(2)}) collective-permute-start(bf16[2,48,512]{2,1,0:T(8,128)(2,1)S(1)} %pad_maximum_fusion.7), channel_id=1, source_target_pairs={{0,6},{2,0},{4,2},{6,4},{1,7},{3,1},{5,3},{7,5},{8,14},{10,8},{12,... | collective-permute-start | bytes 294920 | tf_op jit(solution)/shard_map/ppermute | solution.py:120
  132.4 0.8 collective-permute-start.16
  133.1 2.7 %collective-permute-done.18.three = bf16[2,48,512]{2,1,0:T(8,128)(2,1)S(1)} collective-permute-done((bf16[2,48,512]{2,1,0:T(8,128)(2,1)S(1)}, bf16[2,48,512]{2,1,0:T(8,128)(2,1)S(1)}, u32[]{:S(2)}, u32[]{:S(2)}) %collective-permute-start.18) | collective-permute-done | bytes 98336 | tf_op jit(solution)/shard_map/ppermute | solution.py:120
  135.8 1.8 collective-permute-done.17.two
  137.6 2.3 %collective-permute-done.16.one = bf16[2,48,512]{2,1,0:T(8,128)(2,1)S(1)} collective-permute-done((bf16[2,48,512]{2,1,0:T(8,128)(2,1)S(1)}, bf16[2,48,512]{2,1,0:T(8,128)(2,1)S(1)}, u32[]{:S(2)}, u32[]{:S(2)}) %collective-permute-start.16) | collective-permute-done | bytes 98336 | tf_op jit(solution)/shard_map/ppermute | solution.py:120
  139.9 1.2 collect.3.refs_0_
  141.1 0.9 collective-permute-start.23
  142.9 5.2 %collective-permute-done.23 = bf16[8,48,512]{2,1,0:T(8,128)(2,1)S(1)} collective-permute-done((bf16[8,48,512]{2,1,0:T(8,128)(2,1)S(1)}, bf16[8,48,512]{2,1,0:T(8,128)(2,1)S(1)}, u32[]{:S(2)}, u32[]{:S(2)}) %collective-permute-start.23) | collective-permute-done | bytes 393248 | tf_op jit(solution)/shard_map/ppermute | solution.py:221
  148.6 2.5 %collective-permute-start.30 = (bf16[16,48,512]{2,1,0:T(8,128)(2,1)S(1)}, bf16[16,48,512]{2,1,0:T(8,128)(2,1)S(1)}, u32[]{:S(2)}, u32[]{:S(2)}) collective-permute-start(bf16[16,48,512]{2,1,0:T(8,128)(2,1)S(1)} %collective-permute-done.19.refs_1_.refs_2_), channel_id=1, source_target_pairs={{0,8},{8,0},{1,9},{9,1},{2,10},{10,2},{3,11},{11,3},{4,12},{12,4},... | collective-permute-start | bytes 2359304 | tf_op jit(solution)/shard_map/ppermute | solution.py:236
  151.1 1.7 collective-permute-done.20
  152.8 0.6 collective-permute-start.21
  153.5 10.6 %collective-permute-done.21 = bf16[8,48,512]{2,1,0:T(8,128)(2,1)S(1)} collective-permute-done((bf16[8,48,512]{2,1,0:T(8,128)(2,1)S(1)}, bf16[8,48,512]{2,1,0:T(8,128)(2,1)S(1)}, u32[]{:S(2)}, u32[]{:S(2)}) %collective-permute-start.21) | collective-permute-done | bytes 393248 | tf_op jit(solution)/shard_map/ppermute | solution.py:221
  164.0 1.5 collective-permute-start.24
  166.1 1.1 collective-permute-start.27
  167.8 0.8 collective-permute-done.32.refs_7_
  168.5 3.9 %place_0.1 = (bf16[8,16,96,512]{3,2,1,0:T(8,128)(2,1)}, f32[8,128]{1,0:T(8,128)}) custom-call(s32[5]{0:T(128)S(1)} %stack.41.where.refs_0_, bf16[16,48,512]{2,1,0:T(8,128)(2,1)S(1)} %pad_maximum_fusion.refs_1_.refs_0_, bf16[16,48,512]{2,1,0:T(8,128)(2,1)S(1)} %collective-permute-done.29.refs_1_, ...), custom_call_target="tpu_custom_call" | custom-call | tf_op jit(solution)/shard_map/place_0/pallas_call | solution.py:176
  172.5 2.8 %place_1.2 = (bf16[8,16,96,512]{3,2,1,0:T(8,128)(2,1)}, f32[8,128]{1,0:T(8,128)S(1)}) custom-call(s32[5]{0:T(128)S(1)} %stack.41.where.refs_0_, bf16[16,48,512]{2,1,0:T(8,128)(2,1)S(1)} %pad_maximum_fusion.1.refs_0_, bf16[16,48,512]{2,1,0:T(8,128)(2,1)S(1)} %collective-permute-done.24.refs_1_, ...), custom_call_target="tpu_custom_call", output_to_operand_aliasing={{0}: (7, {})} | custom-call | tf_op jit(solution)/shard_map/place_1/pallas_call | solution.py:176
  175.3 3.9 %collective-permute-done.22.refs_0_ = bf16[16,48,512]{2,1,0:T(8,128)(2,1)S(1)} collective-permute-done((bf16[16,48,512]{2,1,0:T(8,128)(2,1)S(1)}, bf16[16,48,512]{2,1,0:T(8,128)(2,1)S(1)}, u32[]{:S(2)}, u32[]{:S(2)}) %collective-permute-start.22) | collective-permute-done | bytes 786464 | tf_op jit(solution)/shard_map/ppermute | solution.py:221
  179.3 2.3 %collective-permute-done.33.refs_1_ = bf16[16,48,512]{2,1,0:T(8,128)(2,1)S(1)} collective-permute-done((bf16[16,48,512]{2,1,0:T(8,128)(2,1)S(1)}, bf16[16,48,512]{2,1,0:T(8,128)(2,1)S(1)}, u32[]{:S(2)}, u32[]{:S(2)}) %collective-permute-start.33) | collective-permute-done | bytes 786464 | tf_op jit(solution)/shard_map/ppermute | solution.py:236
  181.6 2.3 %place_1.3 = (bf16[8,16,96,512]{3,2,1,0:T(8,128)(2,1)}, f32[8,128]{1,0:T(8,128)}) custom-call(s32[5]{0:T(128)S(1)} %stack.41.where.refs_0_, bf16[16,48,512]{2,1,0:T(8,128)(2,1)S(1)} %after.17.refs_0_, bf16[16,48,512]{2,1,0:T(8,128)(2,1)S(1)} %collective-permute-done.33.refs_1_, ...), custom_call_target="tpu_custom_call", output_to_operand_aliasing={{0}: (3, {})} | custom-call | tf_op jit(solution)/shard_map/place_1/pallas_call | solution.py:176
  (82 shorter events, 9.6 us)
Async XLA Ops:
  17.9 11.8 %collective-permute-start = (f16[384,4096]{1,0:T(8,128)(2,1)S(1)}, f16[384,4096]{1,0:T(8,128)(2,1)S(1)}, u32[]{:S(2)}, u32[]{:S(2)}) collective-permute-start(f16[384,4096]{1,0:T(8,128)(2,1)S(1)} %convolution_convert_fusion.1), channel_id=1, source_target_pairs={{0,8},{8,0},{1,9},{9,1},{2,10},{10,2},{3,11},{11,3},{4,12},{12,4},... | collective-permute-start | bytes 9437192 | tf_op jit(solution)/shard_map/ppermute | solution.py:269
  30.1 20.6 %collective-permute-start.1 = (f16[192,4096]{1,0:T(8,128)(2,1)S(1)}, f16[192,4096]{1,0:T(8,128)(2,1)S(1)}, u32[]{:S(2)}, u32[]{:S(2)}) collective-permute-start(f16[192,4096]{1,0:T(8,128)(2,1)S(1)} %fusion.1), channel_id=1, source_target_pairs={{0,32},{8,104},{32,0},{40,72},{64,96},{72,40},{96,64},{104,8},{1,3... | collective-permute-start | bytes 4718600 | tf_op jit(solution)/shard_map/ppermute | solution.py:221
  43.0 8.6 %copy-start.3 = (bf16[4,2,48,2048]{3,2,1,0:T(8,128)(2,1)S(1)}, bf16[4,2,48,2048]{3,2,1,0:T(8,128)(2,1)}, u32[]{:S(2)}) copy-start(bf16[4,2,48,2048]{3,2,1,0:T(8,128)(2,1)} %get-tuple-element.20) | copy-start | bytes 4718596
  43.0 21.6 %collective-permute-start.2 = (f16[384,4096]{1,0:T(8,128)(2,1)S(1)}, f16[384,4096]{1,0:T(8,128)(2,1)S(1)}, u32[]{:S(2)}, u32[]{:S(2)}) collective-permute-start(f16[384,4096]{1,0:T(8,128)(2,1)S(1)} %convolution_convert_fusion), channel_id=1, source_target_pairs={{0,8},{8,0},{1,9},{9,1},{2,10},{10,2},{3,11},{11,3},{4,12},{12,4},... | collective-permute-start | bytes 9437192 | tf_op jit(solution)/shard_map/ppermute | solution.py:272
  50.9 11.4 %collective-permute-start.4 = (f16[96,4096]{1,0:T(8,128)(2,1)S(1)}, f16[96,4096]{1,0:T(8,128)(2,1)S(1)}, u32[]{:S(2)}, u32[]{:S(2)}) collective-permute-start(f16[96,4096]{1,0:T(8,128)(2,1)S(1)} %fusion.10), channel_id=1, source_target_pairs={{0,96},{8,40},{32,64},{40,8},{64,32},{72,104},{96,0},{104,72},{1,9... | collective-permute-start | bytes 2359304 | tf_op jit(solution)/shard_map/ppermute | solution.py:221
  62.8 9.2 %collective-permute-start.5 = (f16[48,4096]{1,0:T(8,128)(2,1)S(1)}, f16[48,4096]{1,0:T(8,128)(2,1)S(1)}, u32[]{:S(2)}, u32[]{:S(2)}) collective-permute-start(f16[48,4096]{1,0:T(8,128)(2,1)S(1)} %slice_convert_fusion.1), channel_id=1, source_target_pairs={{0,16},{16,0},{1,17},{17,1},{2,18},{18,2},{3,19},{19,3},{4,20},{20... | collective-permute-start | bytes 1179656 | tf_op jit(solution)/shard_map/ppermute | solution.py:263
  64.6 7.5 %copy-start.2 = (f32[1,96,4096]{2,1,0:T(8,128)S(1)}, f32[1,96,4096]{2,1,0:T(8,128)}, u32[]{:S(2)}) copy-start(f32[1,96,4096]{2,1,0:T(8,128)} %param.9) | copy-start | bytes 4718596
  65.0 20.6 %collective-permute-start.3 = (f16[192,4096]{1,0:T(8,128)(2,1)S(1)}, f16[192,4096]{1,0:T(8,128)(2,1)S(1)}, u32[]{:S(2)}, u32[]{:S(2)}) collective-permute-start(f16[192,4096]{1,0:T(8,128)(2,1)S(1)} %fusion), channel_id=1, source_target_pairs={{0,32},{8,104},{32,0},{40,72},{64,96},{72,40},{96,64},{104,8},{1,3... | collective-permute-start | bytes 4718600 | tf_op jit(solution)/shard_map/ppermute | solution.py:221
  67.6 4.5 %copy-start = (f32[1,96,4096]{2,1,0:T(8,128)S(1)}, f32[1,96,4096]{2,1,0:T(8,128)}, u32[]{:S(2)}) copy-start(f32[1,96,4096]{2,1,0:T(8,128)} %param.7) | copy-start | bytes 4718596
  67.6 4.5 %copy-start.1 = (f32[1,96,4096]{2,1,0:T(8,128)S(1)}, f32[1,96,4096]{2,1,0:T(8,128)}, u32[]{:S(2)}) copy-start(f32[1,96,4096]{2,1,0:T(8,128)} %param.8) | copy-start | bytes 4718596
  75.5 10.7 %collective-permute-start.8 = (bf16[4,48,512]{2,1,0:T(8,128)(2,1)S(1)}, bf16[4,48,512]{2,1,0:T(8,128)(2,1)S(1)}, u32[]{:S(2)}, u32[]{:S(2)}) collective-permute-start(bf16[4,48,512]{2,1,0:T(8,128)(2,1)S(1)} %slice_bitcast_fusion.1), channel_id=1, source_target_pairs={{0,1},{1,0},{2,3},{3,2},{4,5},{5,4},{6,7},{7,6},{8,9},{9,8},{10,11... | collective-permute-start | bytes 589832 | tf_op jit(solution)/shard_map/ppermute | solution.py:118
  85.9 11.2 %collective-permute-start.6 = (f16[96,4096]{1,0:T(8,128)(2,1)S(1)}, f16[96,4096]{1,0:T(8,128)(2,1)S(1)}, u32[]{:S(2)}, u32[]{:S(2)}) collective-permute-start(f16[96,4096]{1,0:T(8,128)(2,1)S(1)} %fusion.6), channel_id=1, source_target_pairs={{0,96},{8,40},{32,64},{40,8},{64,32},{72,104},{96,0},{104,72},{1,9... | collective-permute-start | bytes 2359304 | tf_op jit(solution)/shard_map/ppermute | solution.py:221
  86.2 4.4 %collective-permute-start.11 = (bf16[2,48,512]{2,1,0:T(8,128)(2,1)S(1)}, bf16[2,48,512]{2,1,0:T(8,128)(2,1)S(1)}, u32[]{:S(2)}, u32[]{:S(2)}) collective-permute-start(bf16[2,48,512]{2,1,0:T(8,128)(2,1)S(1)} %pad_maximum_fusion.4), channel_id=1, source_target_pairs={{0,6},{2,0},{4,2},{6,4},{1,7},{3,1},{5,3},{7,5},{8,14},{10,8},{12,... | collective-permute-start | bytes 294920 | tf_op jit(solution)/shard_map/ppermute | solution.py:120
  89.0 5.1 %collective-permute-start.10 = (bf16[2,48,512]{2,1,0:T(8,128)(2,1)S(1)}, bf16[2,48,512]{2,1,0:T(8,128)(2,1)S(1)}, u32[]{:S(2)}, u32[]{:S(2)}) collective-permute-start(bf16[2,48,512]{2,1,0:T(8,128)(2,1)S(1)} %pad_maximum_fusion.3), channel_id=1, source_target_pairs={{0,4},{2,6},{4,0},{6,2},{1,5},{3,7},{5,1},{7,3},{8,12},{10,14},{12... | collective-permute-start | bytes 294920 | tf_op jit(solution)/shard_map/ppermute | solution.py:120
  89.5 6.0 %collective-permute-start.9 = (bf16[2,48,512]{2,1,0:T(8,128)(2,1)S(1)}, bf16[2,48,512]{2,1,0:T(8,128)(2,1)S(1)}, u32[]{:S(2)}, u32[]{:S(2)}) collective-permute-start(bf16[2,48,512]{2,1,0:T(8,128)(2,1)S(1)} %pad_maximum_fusion.2), channel_id=1, source_target_pairs={{0,2},{2,4},{4,6},{6,0},{1,3},{3,5},{5,7},{7,1},{8,10},{10,12},{12... | collective-permute-start | bytes 294920 | tf_op jit(solution)/shard_map/ppermute | solution.py:120
  97.6 6.7 %collective-permute-start.12 = (bf16[8,48,512]{2,1,0:T(8,128)(2,1)S(1)}, bf16[8,48,512]{2,1,0:T(8,128)(2,1)S(1)}, u32[]{:S(2)}, u32[]{:S(2)}) collective-permute-start(bf16[8,48,512]{2,1,0:T(8,128)(2,1)S(1)} %after.12), channel_id=1, source_target_pairs={{0,96},{8,40},{32,64},{40,8},{64,32},{72,104},{96,0},{104,72},{1,9... | collective-permute-start | bytes 1179656 | tf_op jit(solution)/shard_map/ppermute | solution.py:221
  98.2 9.5 %collective-permute-start.7 = (f16[48,4096]{1,0:T(8,128)(2,1)S(1)}, f16[48,4096]{1,0:T(8,128)(2,1)S(1)}, u32[]{:S(2)}, u32[]{:S(2)}) collective-permute-start(f16[48,4096]{1,0:T(8,128)(2,1)S(1)} %slice_convert_fusion), channel_id=1, source_target_pairs={{0,16},{16,0},{1,17},{17,1},{2,18},{18,2},{3,19},{19,3},{4,20},{20... | collective-permute-start | bytes 1179656 | tf_op jit(solution)/shard_map/ppermute | solution.py:263
  98.4 12.3 %collective-permute-start.14 = (bf16[8,48,512]{2,1,0:T(8,128)(2,1)S(1)}, bf16[8,48,512]{2,1,0:T(8,128)(2,1)S(1)}, u32[]{:S(2)}, u32[]{:S(2)}) collective-permute-start(bf16[8,48,512]{2,1,0:T(8,128)(2,1)S(1)} %after.12), channel_id=1, source_target_pairs={{0,16},{16,0},{1,17},{17,1},{2,18},{18,2},{3,19},{19,3},{4,20},{20... | collective-permute-start | bytes 1179656 | tf_op jit(solution)/shard_map/ppermute | solution.py:225
  104.3 36.7 %collective-permute-start.19 = (bf16[16,48,512]{2,1,0:T(8,128)(2,1)S(1)}, bf16[16,48,512]{2,1,0:T(8,128)(2,1)S(1)}, u32[]{:S(2)}, u32[]{:S(2)}) collective-permute-start(bf16[16,48,512]{2,1,0:T(8,128)(2,1)S(1)} %pad_maximum_fusion.refs_1_.refs_0_), channel_id=1, source_target_pairs={{0,32},{8,104},{32,0},{40,72},{64,96},{72,40},{96,64},{104,8},{1,3... | collective-permute-start | bytes 2359304 | tf_op jit(solution)/shard_map/ppermute | solution.py:221
  110.7 11.7 %collective-permute-start.15 = (bf16[8,48,512]{2,1,0:T(8,128)(2,1)S(1)}, bf16[8,48,512]{2,1,0:T(8,128)(2,1)S(1)}, u32[]{:S(2)}, u32[]{:S(2)}) collective-permute-start(bf16[8,48,512]{2,1,0:T(8,128)(2,1)S(1)} %collective-permute-done.14), channel_id=1, source_target_pairs={{0,96},{8,40},{32,64},{40,8},{64,32},{72,104},{96,0},{104,72},{1,9... | collective-permute-start | bytes 1179656 | tf_op jit(solution)/shard_map/ppermute | solution.py:221
  114.3 14.9 %collective-permute-start.13 = (bf16[4,48,512]{2,1,0:T(8,128)(2,1)S(1)}, bf16[4,48,512]{2,1,0:T(8,128)(2,1)S(1)}, u32[]{:S(2)}, u32[]{:S(2)}) collective-permute-start(bf16[4,48,512]{2,1,0:T(8,128)(2,1)S(1)} %slice_bitcast_fusion), channel_id=1, source_target_pairs={{0,1},{1,0},{2,3},{3,2},{4,5},{5,4},{6,7},{7,6},{8,9},{9,8},{10,11... | collective-permute-start | bytes 589832 | tf_op jit(solution)/shard_map/ppermute | solution.py:118
  122.4 25.8 %collective-permute-start.25 = (bf16[16,48,512]{2,1,0:T(8,128)(2,1)S(1)}, bf16[16,48,512]{2,1,0:T(8,128)(2,1)S(1)}, u32[]{:S(2)}, u32[]{:S(2)}) collective-permute-start(bf16[16,48,512]{2,1,0:T(8,128)(2,1)S(1)} %constant_dynamic-update-slice_fusion.refs_1_.refs_4_), channel_id=1, source_target_pairs={{0,32},{8,104},{32,0},{40,72},{64,96},{72,40},{96,64},{104,8},{1,3... | collective-permute-start | bytes 2359304 | tf_op jit(solution)/shard_map/ppermute | solution.py:221
  129.2 6.6 %collective-permute-start.18 = (bf16[2,48,512]{2,1,0:T(8,128)(2,1)S(1)}, bf16[2,48,512]{2,1,0:T(8,128)(2,1)S(1)}, u32[]{:S(2)}, u32[]{:S(2)}) collective-permute-start(bf16[2,48,512]{2,1,0:T(8,128)(2,1)S(1)} %pad_maximum_fusion.7), channel_id=1, source_target_pairs={{0,6},{2,0},{4,2},{6,4},{1,7},{3,1},{5,3},{7,5},{8,14},{10,8},{12,... | collective-permute-start | bytes 294920 | tf_op jit(solution)/shard_map/ppermute | solution.py:120
  131.9 5.7 %collective-permute-start.17 = (bf16[2,48,512]{2,1,0:T(8,128)(2,1)S(1)}, bf16[2,48,512]{2,1,0:T(8,128)(2,1)S(1)}, u32[]{:S(2)}, u32[]{:S(2)}) collective-permute-start(bf16[2,48,512]{2,1,0:T(8,128)(2,1)S(1)} %pad_maximum_fusion.6), channel_id=1, source_target_pairs={{0,4},{2,6},{4,0},{6,2},{1,5},{3,7},{5,1},{7,3},{8,12},{10,14},{12... | collective-permute-start | bytes 294920 | tf_op jit(solution)/shard_map/ppermute | solution.py:120
  132.4 7.5 %collective-permute-start.16 = (bf16[2,48,512]{2,1,0:T(8,128)(2,1)S(1)}, bf16[2,48,512]{2,1,0:T(8,128)(2,1)S(1)}, u32[]{:S(2)}, u32[]{:S(2)}) collective-permute-start(bf16[2,48,512]{2,1,0:T(8,128)(2,1)S(1)} %pad_maximum_fusion.5), channel_id=1, source_target_pairs={{0,2},{2,4},{4,6},{6,0},{1,3},{3,5},{5,7},{7,1},{8,10},{10,12},{12... | collective-permute-start | bytes 294920 | tf_op jit(solution)/shard_map/ppermute | solution.py:120
  141.1 7.0 %collective-permute-start.23 = (bf16[8,48,512]{2,1,0:T(8,128)(2,1)S(1)}, bf16[8,48,512]{2,1,0:T(8,128)(2,1)S(1)}, u32[]{:S(2)}, u32[]{:S(2)}) collective-permute-start(bf16[8,48,512]{2,1,0:T(8,128)(2,1)S(1)} %after.15), channel_id=1, source_target_pairs={{0,96},{8,40},{32,64},{40,8},{64,32},{72,104},{96,0},{104,72},{1,9... | collective-permute-start | bytes 1179656 | tf_op jit(solution)/shard_map/ppermute | solution.py:221
  142.0 23.5 %collective-permute-start.29 = (bf16[16,48,512]{2,1,0:T(8,128)(2,1)S(1)}, bf16[16,48,512]{2,1,0:T(8,128)(2,1)S(1)}, u32[]{:S(2)}, u32[]{:S(2)}) collective-permute-start(bf16[16,48,512]{2,1,0:T(8,128)(2,1)S(1)} %pad_maximum_fusion.refs_1_.refs_0_), channel_id=1, source_target_pairs={{0,8},{8,0},{1,9},{9,1},{2,10},{10,2},{3,11},{11,3},{4,12},{12,4},... | collective-permute-start | bytes 2359304 | tf_op jit(solution)/shard_map/ppermute | solution.py:236
  142.4 23.2 %collective-permute-start.31 = (bf16[16,48,512]{2,1,0:T(8,128)(2,1)S(1)}, bf16[16,48,512]{2,1,0:T(8,128)(2,1)S(1)}, u32[]{:S(2)}, u32[]{:S(2)}) collective-permute-start(bf16[16,48,512]{2,1,0:T(8,128)(2,1)S(1)} %constant_dynamic-update-slice_fusion.refs_1_.refs_4_), channel_id=1, source_target_pairs={{0,8},{8,0},{1,9},{9,1},{2,10},{10,2},{3,11},{11,3},{4,12},{12,4},... | collective-permute-start | bytes 2359304 | tf_op jit(solution)/shard_map/ppermute | solution.py:236
  142.5 10.3 %collective-permute-start.20 = (bf16[8,48,512]{2,1,0:T(8,128)(2,1)S(1)}, bf16[8,48,512]{2,1,0:T(8,128)(2,1)S(1)}, u32[]{:S(2)}, u32[]{:S(2)}) collective-permute-start(bf16[8,48,512]{2,1,0:T(8,128)(2,1)S(1)} %after.15), channel_id=1, source_target_pairs={{0,16},{16,0},{1,17},{17,1},{2,18},{18,2},{3,19},{19,3},{4,20},{20... | collective-permute-start | bytes 1179656 | tf_op jit(solution)/shard_map/ppermute | solution.py:225
  148.3 17.9 %collective-permute-start.26 = (bf16[16,48,512]{2,1,0:T(8,128)(2,1)S(1)}, bf16[16,48,512]{2,1,0:T(8,128)(2,1)S(1)}, u32[]{:S(2)}, u32[]{:S(2)}) collective-permute-start(bf16[16,48,512]{2,1,0:T(8,128)(2,1)S(1)} %after.16), channel_id=1, source_target_pairs={{0,32},{8,104},{32,0},{40,72},{64,96},{72,40},{96,64},{104,8},{1,3... | collective-permute-start | bytes 2359304 | tf_op jit(solution)/shard_map/ppermute | solution.py:221
  148.6 18.6 %collective-permute-start.30 = (bf16[16,48,512]{2,1,0:T(8,128)(2,1)S(1)}, bf16[16,48,512]{2,1,0:T(8,128)(2,1)S(1)}, u32[]{:S(2)}, u32[]{:S(2)}) collective-permute-start(bf16[16,48,512]{2,1,0:T(8,128)(2,1)S(1)} %collective-permute-done.19.refs_1_.refs_2_), channel_id=1, source_target_pairs={{0,8},{8,0},{1,9},{9,1},{2,10},{10,2},{3,11},{11,3},{4,12},{12,4},... | collective-permute-start | bytes 2359304 | tf_op jit(solution)/shard_map/ppermute | solution.py:236
  152.8 11.2 %collective-permute-start.21 = (bf16[8,48,512]{2,1,0:T(8,128)(2,1)S(1)}, bf16[8,48,512]{2,1,0:T(8,128)(2,1)S(1)}, u32[]{:S(2)}, u32[]{:S(2)}) collective-permute-start(bf16[8,48,512]{2,1,0:T(8,128)(2,1)S(1)} %collective-permute-done.20), channel_id=1, source_target_pairs={{0,96},{8,40},{32,64},{40,8},{64,32},{72,104},{96,0},{104,72},{1,9... | collective-permute-start | bytes 1179656 | tf_op jit(solution)/shard_map/ppermute | solution.py:221
  164.0 8.4 %collective-permute-start.24 = (bf16[16,48,512]{2,1,0:T(8,128)(2,1)S(1)}, bf16[16,48,512]{2,1,0:T(8,128)(2,1)S(1)}, u32[]{:S(2)}, u32[]{:S(2)}) collective-permute-start(bf16[16,48,512]{2,1,0:T(8,128)(2,1)S(1)} %pad_maximum_fusion.1.refs_0_), channel_id=1, source_target_pairs={{0,8},{8,0},{1,9},{9,1},{2,10},{10,2},{3,11},{11,3},{4,12},{12,4},... | collective-permute-start | bytes 2359304 | tf_op jit(solution)/shard_map/ppermute | solution.py:236
  165.5 3.0 %collective-permute-start.32 = (bf16[16,48,512]{2,1,0:T(8,128)(2,1)S(1)}, bf16[16,48,512]{2,1,0:T(8,128)(2,1)S(1)}, u32[]{:S(2)}, u32[]{:S(2)}) collective-permute-start(bf16[16,48,512]{2,1,0:T(8,128)(2,1)S(1)} %collective-permute-done.25.refs_1_.refs_6_), channel_id=1, source_target_pairs={{0,8},{8,0},{1,9},{9,1},{2,10},{10,2},{3,11},{11,3},{4,12},{12,4},... | collective-permute-start | bytes 2359304 | tf_op jit(solution)/shard_map/ppermute | solution.py:236
  165.6 6.8 %collective-permute-start.28 = (bf16[16,48,512]{2,1,0:T(8,128)(2,1)S(1)}, bf16[16,48,512]{2,1,0:T(8,128)(2,1)S(1)}, u32[]{:S(2)}, u32[]{:S(2)}) collective-permute-start(bf16[16,48,512]{2,1,0:T(8,128)(2,1)S(1)} %constant_dynamic-update-slice_fusion.2.refs_8_.refs_4_), channel_id=1, source_target_pairs={{0,8},{8,0},{1,9},{9,1},{2,10},{10,2},{3,11},{11,3},{4,12},{12,4},... | collective-permute-start | bytes 2359304 | tf_op jit(solution)/shard_map/ppermute | solution.py:236
  166.1 6.4 %collective-permute-start.27 = (bf16[16,48,512]{2,1,0:T(8,128)(2,1)S(1)}, bf16[16,48,512]{2,1,0:T(8,128)(2,1)S(1)}, u32[]{:S(2)}, u32[]{:S(2)}) collective-permute-start(bf16[16,48,512]{2,1,0:T(8,128)(2,1)S(1)} %collective-permute-done.26.refs_2_), channel_id=1, source_target_pairs={{0,8},{8,0},{1,9},{9,1},{2,10},{10,2},{3,11},{11,3},{4,12},{12,4},... | collective-permute-start | bytes 2359304 | tf_op jit(solution)/shard_map/ppermute | solution.py:236
  167.2 12.1 %collective-permute-start.22 = (bf16[16,48,512]{2,1,0:T(8,128)(2,1)S(1)}, bf16[16,48,512]{2,1,0:T(8,128)(2,1)S(1)}, u32[]{:S(2)}, u32[]{:S(2)}) collective-permute-start(bf16[16,48,512]{2,1,0:T(8,128)(2,1)S(1)} %constant_dynamic-update-slice_fusion.2.refs_8_.refs_4_), channel_id=1, source_target_pairs={{0,32},{8,104},{32,0},{40,72},{64,96},{72,40},{96,64},{104,8},{1,3... | collective-permute-start | bytes 2359304 | tf_op jit(solution)/shard_map/ppermute | solution.py:221
  179.3 2.3 %collective-permute-start.33 = (bf16[16,48,512]{2,1,0:T(8,128)(2,1)S(1)}, bf16[16,48,512]{2,1,0:T(8,128)(2,1)S(1)}, u32[]{:S(2)}, u32[]{:S(2)}) collective-permute-start(bf16[16,48,512]{2,1,0:T(8,128)(2,1)S(1)} %after.17.refs_0_), channel_id=1, source_target_pairs={{0,8},{8,0},{1,9},{9,1},{2,10},{10,2},{3,11},{11,3},{4,12},{12,4},... | collective-permute-start | bytes 2359304 | tf_op jit(solution)/shard_map/ppermute | solution.py:236
